TPU v7x, 512 devices: a whole 4x8x8 slice. The times are simulated.
512 devices in a mesh: space: 64 (over x, z, y_lo), rep: 8 (over y_hi, core).
Axes of the slice: x: 4, y: 8 (y_hi: 4, y_lo: 2; y = y_hi * 2 + y_lo), z: 8, core: 2. Of those that a mesh axis runs over, the one named last changes fastest.
Arguments:
- voxels: bfloat16 [8, 128, 8, 8, 8, 96], P('rep', 'space'), may hold values from -6 to 6
- cotangent: bfloat16 [8, 128, 8, 8, 8, 96], P('rep', 'space'), may hold values from -6 to 6
- weight_first: bfloat16 [27, 96, 96], replicated, may hold values from -0.125 to 0.125
- weight_second: bfloat16 [27, 96, 96], replicated, may hold values from -0.125 to 0.125
- act_count: int32 [8, 64], P('rep', 'space'), may hold values from 1 to 2, as said below
- up_list: int32 [8, 64], P('rep', 'space'), may hold values from 0 to 2, as said below
- down_list: int32 [8, 64], P('rep', 'space'), may hold values from 0 to 2, as said below
- table: int32 [8, 128, 9], P('rep', 'space'), may hold values from 0 to 3, as said below
Outputs:
- out_field: bfloat16 [8, 128, 8, 8, 8, 96], P('rep', 'space')
- grad_first: float32 [27, 96, 96], replicated
- grad_second: float32 [27, 96, 96], replicated
Inputs may be any that keep to these rules, and one draw needn't show every extreme that they name: Slots 0 to act_count - 1 of an owner hold its active bricks. In every tile one owner holds 2 active bricks and every other owner at most 1. `up_list`: entry r is the slot of the owner's r-th active brick at local brick x = 1, in increasing y; 2 after the last one. `down_list`: entry r is the slot of the owner's r-th active brick at local brick x = 0, in increasing y; 2 after the last one. `table`: slot p of an owner at local brick position (x, y), x in 0..1, y in 0..0, and direction (dx, dy): the neighbouring position's active brick within the owner (its slot), or in owner o-1 (dx = -1) or o+1 (dx = +1) as 2 + its rank in that owner's up_list or down_list; 3 where no active brick is there, outside the tile, or beyond the first and last owner. Each tile is one brick high.
All inputs are finite; a program needn't handle non-finite values.
Results may differ from a plain program's by a relative error of at most 0.0029.
Values may be sent and summed in bfloat16 or wider, within the bound.
A program may use at most 128 MiB of HBM per device.

v0:
```python
import math

import jax
import jax.numpy as jnp
from jax import lax
from jax.sharding import PartitionSpec as P


def from_behind(block, axis, distance):
    devices = range(lax.axis_size(axis))
    route = [(i - distance, i) for i in devices if i - distance in devices]
    return lax.ppermute(block, axis, route)


def face_planes(field, plane, listing):
    blank_row = jnp.zeros((1,) + field.shape[2:], field.dtype)
    return jnp.take(jnp.concatenate([field[:, plane], blank_row], axis=0), listing, axis=0)


def assemble(field, from_lower, from_upper, links):
    brick_edge = field.shape[1]
    x_blocks = []
    for step_x in (-1, 0, 1):
        y_blocks = []
        for step_y in (-1, 0, 1):
            y_start, y_stop = ((brick_edge - 1, brick_edge), (0, brick_edge), (0, 1))[step_y + 1]
            if step_x == 0:
                own_piece = field[:, :, y_start:y_stop]
                far_piece = jnp.zeros((from_lower.shape[0],) + own_piece.shape[1:], field.dtype)
            elif step_x < 0:
                own_piece = field[:, brick_edge - 1 : brick_edge, y_start:y_stop]
                far_piece = from_lower[:, None, y_start:y_stop]
            else:
                own_piece = field[:, 0:1, y_start:y_stop]
                far_piece = from_upper[:, None, y_start:y_stop]
            blank_row = jnp.zeros((1,) + own_piece.shape[1:], field.dtype)
            sources = jnp.concatenate([own_piece, far_piece, blank_row], axis=0)
            y_blocks.append(jnp.take(sources, links[:, (step_x + 1) * 3 + step_y + 1], axis=0))
        x_blocks.append(jnp.concatenate(y_blocks, axis=2))
    block = jnp.concatenate(x_blocks, axis=1)
    return jnp.pad(block, ((0, 0), (0, 0), (0, 0), (1, 1), (0, 0)))


def depth_rows(padded, offset_x, offset_y):
    brick_edge = padded.shape[1] - 2
    width_in = padded.shape[-1]
    slab = padded[:, offset_x : offset_x + brick_edge, offset_y : offset_y + brick_edge]
    joined = jnp.concatenate(
        [slab[:, :, :, depth : depth + brick_edge] for depth in range(3)], axis=-1
    )
    return joined.reshape(-1, 3 * width_in)


def convolve(padded, weight):
    brick_count = padded.shape[0]
    brick_edge = padded.shape[1] - 2
    width_in = padded.shape[-1]
    summed = None
    for pair in range(9):
        offset_x, offset_y = (pair // 3, pair % 3)
        stacked = weight[3 * pair : 3 * pair + 3].reshape(3 * width_in, -1)
        product = jnp.dot(
            depth_rows(padded, offset_x, offset_y), stacked, preferred_element_type=jnp.float32
        )
        summed = product if summed is None else summed + product
    return summed.reshape(brick_count, brick_edge, brick_edge, brick_edge, -1)


def weight_terms(padded, grads):
    width_in = padded.shape[-1]
    flat_grads = grads.reshape(-1, grads.shape[-1])
    terms = []
    for pair in range(9):
        offset_x, offset_y = (pair // 3, pair % 3)
        block = lax.dot_general(
            depth_rows(padded, offset_x, offset_y),
            flat_grads,
            (((0,), (0,)), ((), ())),
            preferred_element_type=jnp.float32,
        )
        terms.append(block.reshape(3, width_in, -1))
    return jnp.concatenate(terms, axis=0)


def silu_slope(value):
    sigmoid = jax.nn.sigmoid(value)
    return sigmoid * (1.0 + value * (1.0 - sigmoid))


def on_device(voxels, cotangent, weight_first, weight_second, act_count, up_list, down_list, table):
    slot_count = voxels.shape[1]
    brick_edge = voxels.shape[2]
    upward_list = up_list[0]
    downward_list = down_list[0]
    links = table[0]
    live = jnp.arange(slot_count, dtype=jnp.int32) < act_count[0, 0]
    live_mask = live.astype(jnp.float32).reshape(-1, 1, 1, 1, 1)

    def surround(field):
        upward = face_planes(field, brick_edge - 1, upward_list)
        downward = face_planes(field, 0, downward_list)
        from_lower = from_behind(upward, "space", 1)
        from_upper = from_behind(downward, "space", -1)
        return assemble(field, from_lower, from_upper, links)

    inputs = voxels[0] * live_mask.astype(jnp.bfloat16)
    x_pad = surround(inputs)
    before = convolve(x_pad, weight_first) * live_mask
    hidden = jax.nn.silu(before).astype(jnp.bfloat16)
    h_pad = surround(hidden)
    out_field = ((convolve(h_pad, weight_second) + inputs.astype(jnp.float32)) * live_mask).astype(
        jnp.bfloat16
    )
    cotangent_live = cotangent[0] * live_mask.astype(jnp.bfloat16)
    g_pad = surround(cotangent_live)
    second = weight_terms(h_pad, cotangent_live)
    flipped = jnp.swapaxes(weight_second[::-1], 1, 2)
    through = convolve(g_pad, flipped) * live_mask
    slope = (through * silu_slope(before)).astype(jnp.bfloat16)
    first = weight_terms(x_pad, slope)
    first, second = lax.psum((first, second), ("space", "rep"))
    scale = 1.0 / math.sqrt(
        lax.axis_size("space") * lax.axis_size("rep") * slot_count * brick_edge**3
    )
    return (out_field[None], first * scale, second * scale)


def solution(mesh):
    in_specs = (
        P("rep", "space", None, None, None, None),
        P("rep", "space", None, None, None, None),
        P(),
        P(),
        P("rep", "space"),
        P("rep", "space"),
        P("rep", "space"),
        P("rep", "space", None),
    )
    out_specs = (P("rep", "space", None, None, None, None), P(), P())
    return jax.shard_map(
        on_device, mesh=mesh, in_specs=in_specs, out_specs=out_specs, check_vma=False
    )
```

profile of v0, /device:TPU:1, one launch (start us, length us, event | category | flops | bytes accessed | tf_op | source)
XLA Modules:
  0.0 455.1 jit_solution(10137340225588092802)
XLA Ops:
  8.6 1.1 bitcast_multiply_fusion
  9.8 1.3 collective-permute-start.5
  11.8 4.7 %collective-permute-start.4 = (bf16[1,8,8,96]{3,2,1,0:T(8,128)(2,1)S(1)}, bf16[1,8,8,96]{3,2,1,0:T(8,128)(2,1)S(1)}, u32[]{:S(2)}, u32[]{:S(2)}) collective-permute-start(bf16[1,8,8,96]{3,2,1,0:T(8,128)(2,1)S(1)} %fusion.42), channel_id=1, source_target_pairs={{0,8},{8,16},{16,24},{24,32},{32,40},{40,48},{48,56},{56,64},{64,7... | collective-permute-start | bytes 36872 | tf_op jit(solution)/shard_map/ppermute | solution.py:12
  16.6 1.3 collective-permute-start.1
  17.9 4.9 %collective-permute-start = (bf16[1,8,8,96]{3,2,1,0:T(8,128)(2,1)S(1)}, bf16[1,8,8,96]{3,2,1,0:T(8,128)(2,1)S(1)}, u32[]{:S(2)}, u32[]{:S(2)}) collective-permute-start(bf16[1,8,8,96]{3,2,1,0:T(8,128)(2,1)S(1)} %fusion.38), channel_id=1, source_target_pairs={{0,8},{8,16},{16,24},{24,32},{32,40},{40,48},{48,56},{56,64},{64,7... | collective-permute-start | bytes 36872 | tf_op jit(solution)/shard_map/ppermute | solution.py:12
  30.7 1.2 gather_fusion.21
  31.8 1.3 gather_fusion.22
  47.3 1.1 fusion.33
  51.2 1.1 convolution_add_fusion.16
  52.3 2.0 copy.78
  54.3 1.3 multiply_convert_fusion.1
  57.8 1.3 gather_fusion.12
  60.5 1.3 fusion.41
  61.8 1.5 collective-permute-start.3
  63.3 2.4 gather_fusion.13
  65.7 1.5 bitcast_select_fusion.3
  67.2 1.9 broadcast_select_fusion
  69.7 2.2 copy.94
  72.0 2.2 copy.109
  74.2 2.2 copy.110
  76.4 2.2 copy.114
  78.6 2.2 copy.115
  80.8 1.1 copy.116
  81.9 1.1 copy.112
  83.1 1.1 copy.113
  84.1 1.1 copy.111
  86.6 4.9 %collective-permute-start.2 = (bf16[1,8,8,96]{3,2,1,0:T(8,128)(2,1)S(1)}, bf16[1,8,8,96]{3,2,1,0:T(8,128)(2,1)S(1)}, u32[]{:S(2)}, u32[]{:S(2)}) collective-permute-start(bf16[1,8,8,96]{3,2,1,0:T(8,128)(2,1)S(1)} %copy-done.90), channel_id=1, source_target_pairs={{0,8},{8,16},{16,24},{24,32},{32,40},{40,48},{48,56},{56,64},{64,7... | collective-permute-start | bytes 36872 | tf_op jit(solution)/shard_map/ppermute | solution.py:12
  103.2 2.1 fusion.48
  105.8 1.1 copy.117
  107.3 1.1 copy.119
  108.4 1.5 pad_maximum_fusion.15
  110.0 1.1 copy.121
  111.1 1.5 pad_maximum_fusion.17
  112.6 1.1 copy.129
  113.7 1.4 pad_maximum_fusion.18
  115.2 1.1 copy.131
  116.7 1.1 copy.133
  117.9 2.8 fusion.29
  120.7 1.1 copy.123
  121.7 1.1 copy.125
  122.8 1.1 copy.127
  125.1 1.2 fusion.67
  135.1 1.1 fusion.25
  148.9 1.1 copy-done.7
  150.0 1.4 convolution_add_fusion.15
  156.2 288.3 %all-reduce.21.cloned.1.call-done = (f32[27,96,96]{2,1,0:T(8,128)}, f32[27,96,96]{2,1,0:T(8,128)}) async-done(((f32[27,96,96]{2,1,0:T(8,128)}, f32[27,96,96]{2,1,0:T(8,128)}), (f32[27,96,96]{2,1,0:T(8,128)}, f32[27,96,96]{2,1,0:T(8,128)})) %all-reduce.21.cloned.1.call-update) | async-done | bytes 1990672 | tf_op jit(solution)/shard_map/psum | solution.py:121
  444.5 2.6 broadcast_multiply_fusion.1
  447.1 1.2 broadcast_multiply_fusion
  (434 shorter events, 69.7 us)
Async XLA Ops:
  7.2 16.2 %copy-start.45 = (bf16[1,2,8,8,8,96]{5,4,3,2,1,0:T(8,128)(2,1)S(1)}, bf16[1,2,8,8,8,96]{5,4,3,2,1,0:T(8,128)(2,1)}, u32[]{:S(2)}) copy-start(bf16[1,2,8,8,8,96]{5,4,3,2,1,0:T(8,128)(2,1)} %param.19) | copy-start | bytes 589828
  7.2 15.6 %copy-start.84 = (s32[1,2,9]{2,1,0:T(2,128)S(1)}, s32[1,2,9]{2,1,0:T(2,128)}, u32[]{:S(2)}) copy-start(s32[1,2,9]{2,1,0:T(2,128)} %param.25) | copy-start | bytes 220
  7.2 16.3 %copy-start.22 = (bf16[27,96,96]{2,1,0:T(8,128)(2,1)S(1)}, bf16[27,96,96]{2,1,0:T(8,128)(2,1)}, u32[]{:S(2)}) copy-start(bf16[27,96,96]{2,1,0:T(8,128)(2,1)} %param.21) | copy-start | bytes 1492996
  7.2 437.3 %all-reduce.21.cloned.1.call-start = ((), (), s32[]{:S(2)}) async-start(), calls=%async_computation | async-start | bytes 5308416 | tf_op jit(solution)/shard_map/psum | solution.py:121
  8.6 14.8 %copy-start.103 = (bf16[2]{0:T(256)(128)(2,1)}, bf16[2]{0:T(256)(128)(2,1)S(1)}, u32[]{:S(2)}) copy-start(bf16[2]{0:T(256)(128)(2,1)S(1)} %get-tuple-element.225) | copy-start | bytes 16
  8.6 21.2 %copy-start.105 = (f32[2]{0:T(128)}, f32[2]{0:T(128)S(1)}, u32[]{:S(2)}) copy-start(f32[2]{0:T(128)S(1)} %get-tuple-element.224) | copy-start | bytes 28
  9.8 23.3 %collective-permute-start.5 = (bf16[1,8,8,96]{3,2,1,0:T(8,128)(2,1)S(1)}, bf16[1,8,8,96]{3,2,1,0:T(8,128)(2,1)S(1)}, u32[]{:S(2)}, u32[]{:S(2)}) collective-permute-start(bf16[1,8,8,96]{3,2,1,0:T(8,128)(2,1)S(1)} %fusion.43), channel_id=1, source_target_pairs={{8,0},{16,8},{24,16},{32,24},{40,32},{48,40},{56,48},{64,56},{72,6... | collective-permute-start | bytes 36872 | tf_op jit(solution)/shard_map/ppermute | solution.py:12
  11.8 21.4 %collective-permute-start.4 = (bf16[1,8,8,96]{3,2,1,0:T(8,128)(2,1)S(1)}, bf16[1,8,8,96]{3,2,1,0:T(8,128)(2,1)S(1)}, u32[]{:S(2)}, u32[]{:S(2)}) collective-permute-start(bf16[1,8,8,96]{3,2,1,0:T(8,128)(2,1)S(1)} %fusion.42), channel_id=1, source_target_pairs={{0,8},{8,16},{16,24},{24,32},{32,40},{40,48},{48,56},{56,64},{64,7... | collective-permute-start | bytes 36872 | tf_op jit(solution)/shard_map/ppermute | solution.py:12
  16.6 16.6 %collective-permute-start.1 = (bf16[1,8,8,96]{3,2,1,0:T(8,128)(2,1)S(1)}, bf16[1,8,8,96]{3,2,1,0:T(8,128)(2,1)S(1)}, u32[]{:S(2)}, u32[]{:S(2)}) collective-permute-start(bf16[1,8,8,96]{3,2,1,0:T(8,128)(2,1)S(1)} %fusion.39), channel_id=1, source_target_pairs={{8,0},{16,8},{24,16},{32,24},{40,32},{48,40},{56,48},{64,56},{72,6... | collective-permute-start | bytes 36872 | tf_op jit(solution)/shard_map/ppermute | solution.py:12
  17.9 15.3 %collective-permute-start = (bf16[1,8,8,96]{3,2,1,0:T(8,128)(2,1)S(1)}, bf16[1,8,8,96]{3,2,1,0:T(8,128)(2,1)S(1)}, u32[]{:S(2)}, u32[]{:S(2)}) collective-permute-start(bf16[1,8,8,96]{3,2,1,0:T(8,128)(2,1)S(1)} %fusion.38), channel_id=1, source_target_pairs={{0,8},{8,16},{16,24},{24,32},{32,40},{40,48},{48,56},{56,64},{64,7... | collective-permute-start | bytes 36872 | tf_op jit(solution)/shard_map/ppermute | solution.py:12
  23.1 17.6 %copy-start.122 = (pred[2]{0:T(512)(128)(4,1)}, pred[2]{0:T(512)(128)(4,1)S(1)}, u32[]{:S(2)}) copy-start(pred[2]{0:T(512)(128)(4,1)S(1)} %compare_and_fusion.8) | copy-start | bytes 10
  23.1 5.7 %copy-start.110 = (pred[2]{0:T(512)(128)(4,1)}, pred[2]{0:T(512)(128)(4,1)S(1)}, u32[]{:S(2)}) copy-start(pred[2]{0:T(512)(128)(4,1)S(1)} %get-tuple-element.240) | copy-start | bytes 10
  23.1 16.7 %copy-start.113 = (pred[2]{0:T(512)(128)(4,1)}, pred[2]{0:T(512)(128)(4,1)S(1)}, u32[]{:S(2)}) copy-start(pred[2]{0:T(512)(128)(4,1)S(1)} %get-tuple-element.241) | copy-start | bytes 10
  23.2 6.4 %copy-start.111 = (pred[2]{0:T(512)(128)(4,1)}, pred[2]{0:T(512)(128)(4,1)S(1)}, u32[]{:S(2)}) copy-start(pred[2]{0:T(512)(128)(4,1)S(1)} %get-tuple-element.239) | copy-start | bytes 10
  23.2 6.5 %copy-start.112 = (pred[2]{0:T(512)(128)(4,1)}, pred[2]{0:T(512)(128)(4,1)S(1)}, u32[]{:S(2)}) copy-start(pred[2]{0:T(512)(128)(4,1)S(1)} %get-tuple-element.238) | copy-start | bytes 10
  23.2 15.9 %copy-start.119 = (pred[2]{0:T(512)(128)(4,1)}, pred[2]{0:T(512)(128)(4,1)S(1)}, u32[]{:S(2)}) copy-start(pred[2]{0:T(512)(128)(4,1)S(1)} %get-tuple-element.237) | copy-start | bytes 10
  23.2 16.5 %copy-start.108 = (pred[2]{0:T(512)(128)(4,1)}, pred[2]{0:T(512)(128)(4,1)S(1)}, u32[]{:S(2)}) copy-start(pred[2]{0:T(512)(128)(4,1)S(1)} %get-tuple-element.236) | copy-start | bytes 10
  23.3 16.6 %copy-start.117 = (pred[2]{0:T(512)(128)(4,1)}, pred[2]{0:T(512)(128)(4,1)S(1)}, u32[]{:S(2)}) copy-start(pred[2]{0:T(512)(128)(4,1)S(1)} %get-tuple-element.235) | copy-start | bytes 10
  23.3 17.3 %copy-start.115 = (pred[2]{0:T(512)(128)(4,1)}, pred[2]{0:T(512)(128)(4,1)S(1)}, u32[]{:S(2)}) copy-start(pred[2]{0:T(512)(128)(4,1)S(1)} %get-tuple-element.234) | copy-start | bytes 10
  24.7 11.4 %copy-start.99 = (s32[1024]{0:T(1024)}, s32[1024]{0:T(1024)S(1)}, u32[]{:S(2)}) copy-start(s32[1024]{0:T(1024)S(1)} %pad_clamp_fusion.8) | copy-start | bytes 12292
  24.7 14.5 %copy-start.94 = (s32[1024]{0:T(1024)}, s32[1024]{0:T(1024)S(1)}, u32[]{:S(2)}) copy-start(s32[1024]{0:T(1024)S(1)} %pad_clamp_fusion.1) | copy-start | bytes 12292
  24.7 13.8 %copy-start.102 = (s32[1024]{0:T(1024)}, s32[1024]{0:T(1024)S(1)}, u32[]{:S(2)}) copy-start(s32[1024]{0:T(1024)S(1)} %pad_clamp_fusion.2) | copy-start | bytes 12292
  24.8 7.1 %copy-start.96 = (s32[1024]{0:T(1024)}, s32[1024]{0:T(1024)S(1)}, u32[]{:S(2)}) copy-start(s32[1024]{0:T(1024)S(1)} %pad_clamp_fusion.4) | copy-start | bytes 12292
  24.8 9.1 %copy-start.100 = (s32[1024]{0:T(1024)}, s32[1024]{0:T(1024)S(1)}, u32[]{:S(2)}) copy-start(s32[1024]{0:T(1024)S(1)} %pad_clamp_fusion.6) | copy-start | bytes 12292
  24.8 10.2 %copy-start.101 = (s32[1024]{0:T(1024)}, s32[1024]{0:T(1024)S(1)}, u32[]{:S(2)}) copy-start(s32[1024]{0:T(1024)S(1)} %pad_clamp_fusion) | copy-start | bytes 12292
  24.9 5.8 %copy-start.98 = (s32[1024]{0:T(1024)}, s32[1024]{0:T(1024)S(1)}, u32[]{:S(2)}) copy-start(s32[1024]{0:T(1024)S(1)} %pad_clamp_fusion.5) | copy-start | bytes 12292
  29.6 11.9 %copy-start.17 = (bf16[2,8,8,8,96]{4,3,2,1,0:T(8,128)(2,1)}, bf16[2,8,8,8,96]{4,3,2,1,0:T(8,128)(2,1)S(1)}, u32[]{:S(2)}) copy-start(bf16[2,8,8,8,96]{4,3,2,1,0:T(8,128)(2,1)S(1)} %broadcast_select_fusion.2) | copy-start | bytes 589828
  29.8 10.9 %copy-start.95 = (s32[1024]{0:T(1024)}, s32[1024]{0:T(1024)S(1)}, u32[]{:S(2)}) copy-start(s32[1024]{0:T(1024)S(1)} %pad_clamp_fusion.7) | copy-start | bytes 12292
  33.2 8.8 %copy-start.92 = (bf16[4]{0:T(256)(128)(2,1)}, bf16[4]{0:T(256)(128)(2,1)S(1)}, u32[]{:S(2)}) copy-start(bf16[4]{0:T(256)(128)(2,1)S(1)} %pad.235.clone) | copy-start | bytes 28
  44.9 5.7 %copy-start.11 = (bf16[2,8,8,8,288]{4,3,2,1,0:T(8,128)(2,1)}, bf16[2,8,8,8,288]{4,3,2,1,0:T(8,128)(2,1)S(1)}, u32[]{:S(2)}) copy-start(bf16[2,8,8,8,288]{4,3,2,1,0:T(8,128)(2,1)S(1)} %pad_maximum_fusion.11) | copy-start | bytes 1769476
  45.3 4.8 %copy-start.12 = (bf16[2,8,8,8,288]{4,3,2,1,0:T(8,128)(2,1)}, bf16[2,8,8,8,288]{4,3,2,1,0:T(8,128)(2,1)S(1)}, u32[]{:S(2)}) copy-start(bf16[2,8,8,8,288]{4,3,2,1,0:T(8,128)(2,1)S(1)} %pad_maximum_fusion.10) | copy-start | bytes 1769476
  59.7 9.4 %copy-start.83 = (bf16[2,8,8,96]{3,2,1,0:T(8,128)(2,1)S(1)}, bf16[2,8,8,96]{3,2,1,0:T(8,128)(2,1)}, u32[]{:S(2)}) copy-start(bf16[2,8,8,96]{3,2,1,0:T(8,128)(2,1)} %get-tuple-element.158) | copy-start | bytes 73732
  61.8 29.7 %collective-permute-start.3 = (bf16[1,8,8,96]{3,2,1,0:T(8,128)(2,1)}, bf16[1,8,8,96]{3,2,1,0:T(8,128)(2,1)}, u32[]{:S(2)}, u32[]{:S(2)}) collective-permute-start(bf16[1,8,8,96]{3,2,1,0:T(8,128)(2,1)} %fusion.41), channel_id=1, source_target_pairs={{8,0},{16,8},{24,16},{32,24},{40,32},{48,40},{56,48},{64,56},{72,6... | collective-permute-start | bytes 36872 | tf_op jit(solution)/shard_map/ppermute | solution.py:12
  83.0 9.4 %copy-start.86 = (bf16[2,1,1,8,96]{4,3,2,0,1:T(8,128)(2,1)S(1)}, bf16[2,1,1,8,96]{4,3,2,0,1:T(8,128)(2,1)}, u32[]{:S(2)}) copy-start(bf16[2,1,1,8,96]{4,3,2,0,1:T(8,128)(2,1)} %get-tuple-element.153) | copy-start | bytes 9220
  83.0 9.4 %copy-start.87 = (bf16[2,1,1,8,96]{4,3,2,0,1:T(8,128)(2,1)S(1)}, bf16[2,1,1,8,96]{4,3,2,0,1:T(8,128)(2,1)}, u32[]{:S(2)}) copy-start(bf16[2,1,1,8,96]{4,3,2,0,1:T(8,128)(2,1)} %get-tuple-element.154) | copy-start | bytes 9220
  83.0 9.4 %copy-start.88 = (bf16[2,1,1,8,96]{4,3,2,0,1:T(8,128)(2,1)S(1)}, bf16[2,1,1,8,96]{4,3,2,0,1:T(8,128)(2,1)}, u32[]{:S(2)}) copy-start(bf16[2,1,1,8,96]{4,3,2,0,1:T(8,128)(2,1)} %get-tuple-element.155) | copy-start | bytes 9220
  83.0 9.4 %copy-start.89 = (bf16[2,1,1,8,96]{4,3,2,0,1:T(8,128)(2,1)S(1)}, bf16[2,1,1,8,96]{4,3,2,0,1:T(8,128)(2,1)}, u32[]{:S(2)}) copy-start(bf16[2,1,1,8,96]{4,3,2,0,1:T(8,128)(2,1)} %get-tuple-element.156) | copy-start | bytes 9220
  83.0 9.4 %copy-start.93 = (bf16[4]{0:T(256)(128)(2,1)S(1)}, bf16[4]{0:T(256)(128)(2,1)}, u32[]{:S(2)}) copy-start(bf16[4]{0:T(256)(128)(2,1)} %copy-done.92) | copy-start | bytes 28
  83.0 10.1 %copy-start.81 = (bf16[2,1,8,8,96]{4,3,2,0,1:T(8,128)(2,1)S(1)}, bf16[2,1,8,8,96]{4,3,2,0,1:T(8,128)(2,1)}, u32[]{:S(2)}) copy-start(bf16[2,1,8,8,96]{4,3,2,0,1:T(8,128)(2,1)} %get-tuple-element.157) | copy-start | bytes 73732
  83.0 10.1 %copy-start.82 = (bf16[2,1,8,8,96]{4,3,2,0,1:T(8,128)(2,1)S(1)}, bf16[2,1,8,8,96]{4,3,2,0,1:T(8,128)(2,1)}, u32[]{:S(2)}) copy-start(bf16[2,1,8,8,96]{4,3,2,0,1:T(8,128)(2,1)} %get-tuple-element.160) | copy-start | bytes 73732
  83.0 11.6 %copy-start.120 = (pred[2]{0:T(512)(128)(4,1)S(1)}, pred[2]{0:T(512)(128)(4,1)}, u32[]{:S(2)}) copy-start(pred[2]{0:T(512)(128)(4,1)} %copy-done.119) | copy-start | bytes 10
  83.0 11.7 %copy-start.109 = (pred[2]{0:T(512)(128)(4,1)S(1)}, pred[2]{0:T(512)(128)(4,1)}, u32[]{:S(2)}) copy-start(pred[2]{0:T(512)(128)(4,1)} %copy-done.108) | copy-start | bytes 10
  84.1 10.7 %copy-start.91 = (bf16[2,1,1,8,96]{4,3,2,0,1:T(8,128)(2,1)S(1)}, bf16[2,1,1,8,96]{4,3,2,0,1:T(8,128)(2,1)}, u32[]{:S(2)}) copy-start(bf16[2,1,1,8,96]{4,3,2,0,1:T(8,128)(2,1)} %get-tuple-element.214) | copy-start | bytes 9220
  84.1 10.7 %copy-start.19 = (bf16[2,8,8,8,96]{4,3,2,1,0:T(8,128)(2,1)S(1)}, bf16[2,8,8,8,96]{4,3,2,1,0:T(8,128)(2,1)}, u32[]{:S(2)}) copy-start(bf16[2,8,8,8,96]{4,3,2,1,0:T(8,128)(2,1)} %get-tuple-element.204) | copy-start | bytes 589828
  84.1 10.7 %copy-start.56 = (bf16[2,1,8,8,96]{4,3,2,1,0:T(8,128)(2,1)S(1)}, bf16[2,1,8,8,96]{4,3,2,1,0:T(8,128)(2,1)}, u32[]{:S(2)}) copy-start(bf16[2,1,8,8,96]{4,3,2,1,0:T(8,128)(2,1)} %get-tuple-element.196) | copy-start | bytes 73732
  86.6 5.7 %collective-permute-start.2 = (bf16[1,8,8,96]{3,2,1,0:T(8,128)(2,1)S(1)}, bf16[1,8,8,96]{3,2,1,0:T(8,128)(2,1)S(1)}, u32[]{:S(2)}, u32[]{:S(2)}) collective-permute-start(bf16[1,8,8,96]{3,2,1,0:T(8,128)(2,1)S(1)} %copy-done.90), channel_id=1, source_target_pairs={{0,8},{8,16},{16,24},{24,32},{32,40},{40,48},{48,56},{56,64},{64,7... | collective-permute-start | bytes 36872 | tf_op jit(solution)/shard_map/ppermute | solution.py:12
  94.9 3.7 copy-start.21
  94.9 3.7 copy-start.55
  (83 other events, 129.6 us)
Sparse Core Ops, SparseCore 0:
  149.0 295.3 all-reduce.20
where the time goes:
time: 457 us; the launch traced here: 455 us
  waiting for transfers between devices  288 us (63%)
  local copies, waits for them, and re-layouts  70.7 us (15%)
  other arithmetic  34.9 us (8%)
  matrix products  24.7 us (5%)
  starting transfers between devices  18.5 us (4%)
  between operations  17.8 us (4%)
    psum x1, waiting for transfers between devices, on_device(): first, second = lax.psum((first, second), ('space', 'rep'))  288 us
    gather x27, local copies, waits for them, and re-layouts, assemble(): jnp.take(sources, links[:, (step_x + 1) * 3 + step_y + 1], axis=0)  20.2 us
    ppermute x6, starting transfers between devices, from_behind(): return lax.ppermute(block, axis, route)  18.5 us
    concatenate x21, other arithmetic, depth_rows(): jnp.concatenate([slab[:, :, :, depth:depth + brick_edge] for depth in ran...  15.6 us
    reshape x9, local copies, waits for them, and re-layouts, depth_rows(): return joined.reshape(-1, 3 * width_in)  15.4 us
    dot_general x27, matrix products, convolve(): jnp.dot(depth_rows(padded, offset_x, offset_y), stacked, preferred_elemen...  12.9 us
    dot_general x18, matrix products, weight_terms(): lax.dot_general(depth_rows(padded, offset_x, offset_y), flat_grads, (((0,...  11.9 us
    dot_general x9, local copies, waits for them, and re-layouts, weight_terms(): lax.dot_general(depth_rows(padded, offset_x, offset_y), flat_grads, (((0,...  9.92 us
  transfers between devices with their start and end apart: 7, of which 2 were waited for; matrix products, arithmetic and copies ran while one was open for 8% of the time, Pallas kernels for 0%

commit v1 on v0

v1 whole, which is shorter than its diff:
```python
import functools
import math

import jax
import jax.numpy as jnp
from jax import lax
from jax.experimental import pallas as pl
from jax.experimental.pallas import tpu as pltpu
from jax.sharding import PartitionSpec as P

F32 = jnp.float32
BF16 = jnp.bfloat16
MESH = pl.DeviceIdType.MESH

SIZE_X, SIZE_Y, SIZE_Z = 4, 8, 8
EDGE = 8
CH = 96
LANES = 128
FACE = EDGE * EDGE
PLANES = 2 * EDGE
ROWS = PLANES * FACE
WIDE = 9 * CH
TILES_WIDE = 7
HALF = 1024
PART = 128
SHARD = 16
CHUNK = 4
STEP = CHUNK * FACE


def widen(value):
    value = value.astype(F32)
    blank = jnp.zeros(value.shape[:-1] + (LANES - CH,), F32)
    return jnp.concatenate([value, blank], axis=-1)


def spread(value, out, row):
    planes = value.shape[0]
    flat = value.reshape(planes * EDGE, EDGE, LANES)
    depth = lax.broadcasted_iota(jnp.int32, flat.shape, 1)
    by_depth = [
        jnp.where(depth == 0, 0.0, pltpu.roll(flat, 1, 1)),
        flat,
        jnp.where(depth == EDGE - 1, 0.0, pltpu.roll(flat, EDGE - 1, 1)),
    ]

    def piece(index):
        shift_y, shift_z = index // 3, index % 3
        turned = by_depth[shift_z]
        turn = CH * index % LANES
        if turn:
            turned = pltpu.roll(turned, turn, 2)
        turned = turned.reshape(planes, EDGE, EDGE, LANES)
        blank = jnp.zeros((planes, 1, EDGE, LANES), F32)
        if shift_y == 0:
            turned = jnp.concatenate([blank, turned[:, : EDGE - 1]], axis=1)
        elif shift_y == 2:
            turned = jnp.concatenate([turned[:, 1:], blank], axis=1)
        return turned.reshape(planes * FACE, LANES)

    lane = lax.broadcasted_iota(jnp.int32, (planes * FACE, LANES), 1)
    pieces = [piece(index) for index in range(9)]
    for tile in range(TILES_WIDE):
        first = LANES * tile // CH
        border = CH * (first + 1) - LANES * tile
        block = pieces[first]
        if border < LANES and first + 1 < 9:
            block = jnp.where(lane < border, block, pieces[first + 1])
        out[pl.ds(row, planes * FACE), LANES * tile : LANES * (tile + 1)] = block.astype(BF16)


def section(
    scale,
    down_ref, up_ref, vox, cot, w1, w2,
    out, packed,
    ax, ah, ag, wa, wb, wt, dslope, sums, st, ct,
    up_send, down_send, from_lo, from_hi, hup_send, hdown_send, hfrom_lo, hfrom_hi,
    part_sum, core_in, ring_out, ring_in, mid, mid_in, cross,
    halo_s, halo_r, s0, r0, s1, r1, s2, r2, s3, r3, s4, r4, s5, r5, s6, r6,
):
    space = lax.axis_index("space")
    rep = lax.axis_index("rep")
    owners = SIZE_X * SIZE_Z * 2
    y_lo = lax.rem(space, 2)
    my_z = lax.rem(lax.div(space, 2), SIZE_Z)
    my_x = lax.div(space, 2 * SIZE_Z)
    core = lax.rem(rep, 2)
    my_y = lax.div(rep, 2) * 2 + y_lo

    def device(x, y, z, c):
        return ((x * SIZE_Z + z) * 2 + lax.rem(y, 2), lax.div(y, 2) * 2 + c)

    pos1 = my_y * (1 - core) + my_z * core
    pos2 = my_z * (1 - core) + my_y * core

    def ring1(t):
        return device(my_x, t * (1 - core) + my_y * core, my_z * (1 - core) + t * core, core)

    def ring2(t):
        return device(my_x, my_y * (1 - core) + t * core, t * (1 - core) + my_z * core, core)

    def across(t):
        return device(t, my_y, my_z, core)

    twin = device(my_x, my_y, my_z, 1 - core)
    above = (lax.rem(space + 1, owners), rep)
    below = (lax.rem(space + owners - 1, owners), rep)

    def send(src, dst, send_sem, recv_sem, target):
        copy = pltpu.make_async_remote_copy(
            src_ref=src, dst_ref=dst, send_sem=send_sem, recv_sem=recv_sem,
            device_id=target, device_id_type=MESH,
        )
        copy.start()
        return copy

    def arrived(dst, send_sem, recv_sem, target):
        pltpu.make_async_remote_copy(
            src_ref=dst, dst_ref=dst, send_sem=send_sem, recv_sem=recv_sem,
            device_id=target, device_id_type=MESH,
        ).wait_recv()

    barrier = pltpu.get_barrier_semaphore()
    partners = [above, below, twin]
    partners += [ring1(lax.rem(pos1 + d, 8)) for d in range(1, 8)]
    partners += [ring2(lax.rem(pos2 + d, 8)) for d in range(1, 8)]
    partners += [across(lax.rem(my_x + d, SIZE_X)) for d in range(1, SIZE_X)]
    for partner in partners:
        pl.semaphore_signal(barrier, inc=1, device_id=partner, device_id_type=MESH)

    down = down_ref[0, 0]
    up = up_ref[0, 0]
    sent = []

    def face(field, slot, plane):
        first, second = widen(field[0, plane]), widen(field[1, plane])
        chosen = jnp.where(slot == 0, first, jnp.where(slot == 1, second, 0.0))
        return chosen.reshape(FACE, LANES).astype(BF16)

    for at, field in enumerate((vox, cot)):
        up_send[at * FACE : (at + 1) * FACE] = face(field, up, EDGE - 1)
        down_send[at * FACE : (at + 1) * FACE] = face(field, down, 0)
    pl.semaphore_wait(barrier, len(partners))
    sent.append(send(up_send, from_lo, halo_s.at[0], halo_r.at[0], above))
    sent.append(send(down_send, from_hi, halo_s.at[1], halo_r.at[1], below))

    def fill(field, wide):
        def body(c, carry):
            planes = pl.ds(lax.rem(c, 2) * CHUNK, CHUNK)
            slot = jnp.where(c < 2, down, up)
            first, second = widen(field[0, planes]), widen(field[1, planes])
            chosen = jnp.where(slot == 0, first, jnp.where(slot == 1, second, 0.0))
            spread(chosen, wide, pl.multiple_of(FACE + c * STEP, FACE))
            return carry

        lax.fori_loop(0, 4, body, 0)

    fill(vox, ax)

    def weights(o, carry):
        rows = pl.ds(pl.multiple_of(o * CH, CH), CH)
        wa[rows] = widen(w1[o]).astype(BF16)
        own = widen(w2[o])
        wb[rows] = own.astype(BF16)
        square = jnp.concatenate([own, jnp.zeros((LANES - CH, LANES), F32)], axis=0)
        wt[pl.ds(pl.multiple_of((26 - o) * CH, CH), CH)] = square.T[:CH].astype(BF16)
        return carry

    lax.fori_loop(0, 27, weights, 0)
    fill(cot, ag)

    def cot_turn(c, carry):
        block = ag[pl.ds(pl.multiple_of(FACE + c * STEP, FACE), STEP), 3 * LANES : 4 * LANES]
        ct[:, pl.ds(pl.multiple_of(c * STEP, STEP), STEP)] = block.astype(F32).T[:CH].astype(BF16)
        return carry

    lax.fori_loop(0, 4, cot_turn, 0)

    def edge_in(buffer, at, valid, wide, row):
        block = buffer[at * FACE : (at + 1) * FACE].astype(F32)
        block = jnp.where(valid, block, 0.0).reshape(1, EDGE, EDGE, LANES)
        spread(block, wide, row)

    lower_valid = space > 0
    upper_valid = space < owners - 1
    last_row = FACE + ROWS
    arrived(from_lo, halo_s.at[0], halo_r.at[0], above)
    edge_in(from_lo, 0, lower_valid, ax, 0)
    edge_in(from_lo, 1, lower_valid, ag, 0)
    arrived(from_hi, halo_s.at[1], halo_r.at[1], below)
    edge_in(from_hi, 0, upper_valid, ax, last_row)
    edge_in(from_hi, 1, upper_valid, ag, last_row)

    def convolve(wide, weight, c):
        total = None
        for i in range(3):
            rows = pl.ds(pl.multiple_of(c * STEP + i * FACE, FACE), STEP)
            product = jnp.dot(
                wide[rows, :WIDE], weight[i * WIDE : (i + 1) * WIDE], preferred_element_type=F32
            )
            total = product if total is None else total + product
        active = jnp.where(c < 2, down, up) < 2
        return total, active

    def first_conv(c):
        total, active = convolve(ax, wa, c)
        before = jnp.where(active, total, 0.0)
        gate = jax.nn.sigmoid(before)
        dslope[pl.ds(pl.multiple_of(c * STEP, STEP), STEP)] = gate * (1.0 + before * (1.0 - gate))
        hidden = (before * gate).astype(BF16).astype(F32)
        spread(
            hidden.reshape(CHUNK, EDGE, EDGE, LANES), ah, pl.multiple_of(FACE + c * STEP, FACE)
        )

    def both_ends(n, carry):
        first_conv(n * 3)
        return carry

    lax.fori_loop(0, 2, both_ends, 0)
    centre = slice(3 * LANES, 4 * LANES)
    hdown_send[...] = ah[FACE : 2 * FACE, centre]
    hup_send[...] = ah[ROWS : ROWS + FACE, centre]
    sent.append(send(hup_send, hfrom_lo, halo_s.at[2], halo_r.at[2], above))
    sent.append(send(hdown_send, hfrom_hi, halo_s.at[3], halo_r.at[3], below))

    def middle(n, carry):
        first_conv(n + 1)
        return carry

    lax.fori_loop(0, 2, middle, 0)

    def through(c, carry):
        total, active = convolve(ag, wt, c)
        rows = pl.ds(pl.multiple_of(c * STEP, STEP), STEP)
        slope = jnp.where(active, total, 0.0) * dslope[rows]
        st[:, rows] = slope.T[:CH].astype(BF16)
        return carry

    lax.fori_loop(0, 4, through, 0)

    def gradient(turned, wide, g):
        def body(i, carry):
            rows = pl.ds(pl.multiple_of(i * FACE, FACE), ROWS)
            block = jnp.dot(turned[...], wide[rows], preferred_element_type=F32)
            for tile in range(TILES_WIDE):
                at = pl.multiple_of((i * TILES_WIDE + tile) * CH, CH)
                part_sum[g, pl.ds(at, CH)] = block[:, LANES * tile : LANES * (tile + 1)]
            return carry

        lax.fori_loop(0, 3, body, 0)
        used = 3 * TILES_WIDE * CH
        part_sum[g, used:] = jnp.zeros((2 * HALF - used, LANES), F32)

    def rows_of(start, count):
        return pl.ds(pl.multiple_of(start, SHARD), count)

    def core_send(g):
        for t in range(8):
            src = part_sum.at[g, rows_of((1 - core) * HALF + t * PART, PART)]
            sent.append(
                send(src, core_in.at[g, pl.ds(t * PART, PART)], s0.at[g, t], r0.at[g, t], twin)
            )

    def core_add(g):
        for t in range(8):
            arrived(core_in.at[g, pl.ds(t * PART, PART)], s0.at[g, t], r0.at[g, t], twin)
        for d in (4, 3, 5, 2, 6, 1, 7, 0):
            t = lax.rem(pos1 + d, 8)
            total = (
                part_sum[g, rows_of(core * HALF + t * PART, PART)]
                + core_in[g, rows_of(t * PART, PART)]
            )
            if d == 0:
                mid[g] = total
            else:
                ring_out[g, d] = total.astype(BF16)
                sent.append(
                    send(ring_out.at[g, d], ring_in.at[g, d], s1.at[g, d], r1.at[g, d], ring1(t))
                )

    def ring1_add(g):
        for d in range(1, 8):
            arrived(ring_in.at[g, d], s1.at[g, d], r1.at[g, d], twin)
        total = mid[g]
        for d in range(1, 8):
            total = total + ring_in[g, d].astype(F32)
        mid[g] = total
        for d in (4, 3, 5, 2, 6, 1, 7):
            t = lax.rem(pos2 + d, 8)
            src = mid.at[g, rows_of(t * SHARD, SHARD)]
            sent.append(send(src, mid_in.at[g, d], s2.at[g, d], r2.at[g, d], ring2(t)))

    def ring2_add(g):
        for d in range(1, 8):
            arrived(mid_in.at[g, d], s2.at[g, d], r2.at[g, d], twin)
        total = mid[g, rows_of(pos2 * SHARD, SHARD)]
        for d in range(1, 8):
            total = total + mid_in[g, d]
        cross[g, my_x] = total
        for d in (2, 1, 3):
            t = lax.rem(my_x + d, SIZE_X)
            sent.append(
                send(cross.at[g, my_x], cross.at[g, my_x], s3.at[g, d], r3.at[g, d], across(t))
            )

    def cross_add(g):
        for d in range(1, SIZE_X):
            t = lax.rem(my_x + SIZE_X - d, SIZE_X)
            arrived(cross.at[g, t], s3.at[g, d], r3.at[g, d], twin)
        total = cross[g, 0]
        for t in range(1, SIZE_X):
            total = total + cross[g, t]
        mine = rows_of(core * HALF + pos1 * PART + pos2 * SHARD, SHARD)
        packed[g, mine] = (total * scale).astype(BF16)
        for d in (4, 3, 5, 2, 6, 1, 7):
            t = lax.rem(pos2 + d, 8)
            sent.append(
                send(packed.at[g, mine], packed.at[g, mine], s4.at[g, d], r4.at[g, d], ring2(t))
            )

    def ring2_gather(g):
        for d in range(1, 8):
            t = lax.rem(pos2 + 8 - d, 8)
            theirs = rows_of(core * HALF + pos1 * PART + t * SHARD, SHARD)
            arrived(packed.at[g, theirs], s4.at[g, d], r4.at[g, d], twin)
        mine = packed.at[g, rows_of(core * HALF + pos1 * PART, PART)]
        for d in (4, 3, 5, 2, 6, 1, 7):
            t = lax.rem(pos1 + d, 8)
            sent.append(send(mine, mine, s5.at[g, d], r5.at[g, d], ring1(t)))
        sent.append(send(mine, mine, s6.at[g, 0], r6.at[g, 0], twin))

    def ring1_gather(g):
        for d in (1, 7, 2, 6, 3, 5, 4):
            t = lax.rem(pos1 + 8 - d, 8)
            theirs = packed.at[g, rows_of(core * HALF + t * PART, PART)]
            arrived(theirs, s5.at[g, d], r5.at[g, d], twin)
            sent.append(send(theirs, theirs, s6.at[g, d], r6.at[g, d], twin))

    def core_gather(g):
        for d in range(8):
            t = lax.rem(pos2 + 8 - d, 8)
            theirs = packed.at[g, rows_of((1 - core) * HALF + t * PART, PART)]
            arrived(theirs, s6.at[g, d], r6.at[g, d], twin)

    gradient(st, ax, 0)
    core_send(0)
    arrived(hfrom_lo, halo_s.at[2], halo_r.at[2], above)
    edge_in(hfrom_lo, 0, lower_valid, ah, 0)
    arrived(hfrom_hi, halo_s.at[3], halo_r.at[3], below)
    edge_in(hfrom_hi, 0, upper_valid, ah, last_row)
    core_add(0)
    gradient(ct, ah, 1)
    core_send(1)
    core_add(1)

    def second_conv(c, carry):
        total, active = convolve(ah, wb, c)
        inputs = ax[pl.ds(pl.multiple_of(FACE + c * STEP, FACE), STEP), centre].astype(F32)
        rows = pl.ds(pl.multiple_of(c * STEP, STEP), STEP)
        sums[rows] = jnp.where(active, total + inputs, 0.0)
        return carry

    lax.fori_loop(0, 4, second_conv, 0)

    def place(n, carry):
        low = sums[pl.ds(pl.multiple_of(n * STEP, STEP), STEP)]
        high = sums[pl.ds(pl.multiple_of(ROWS // 2 + n * STEP, STEP), STEP)]
        for slot in range(2):
            chosen = jnp.where(down == slot, low, jnp.where(up == slot, high, 0.0))
            chosen = chosen.reshape(CHUNK, EDGE, EDGE, LANES)[..., :CH]
            out[slot, pl.ds(n * CHUNK, CHUNK)] = chosen.astype(BF16)
        return carry

    lax.fori_loop(0, 2, place, 0)

    for stage in (ring1_add, ring2_add, cross_add, ring2_gather, ring1_gather, core_gather):
        for g in range(2):
            stage(g)
    for copy in sent:
        copy.wait_send()


def unpack(packed, field, first, second, out):
    out[...] = field[...]
    for g, result in enumerate((first, second)):
        for tile in range(TILES_WIDE):
            turned = packed[g, CH * tile : CH * (tile + 1)].astype(F32).T
            count = min(LANES, WIDE - LANES * tile)
            result[LANES * tile : LANES * tile + count] = turned[:count]


def on_device(voxels, cotangent, weight_first, weight_second, act_count, up_list, down_list, table):
    vmem = pl.BlockSpec(memory_space=pltpu.VMEM)
    smem = pl.BlockSpec(memory_space=pltpu.SMEM)
    scale = 1.0 / math.sqrt(512 * 2 * EDGE**3)
    dma = pltpu.SemaphoreType.DMA
    field_shape = jax.ShapeDtypeStruct((2, EDGE, EDGE, EDGE, CH), BF16)
    packed_shape = jax.ShapeDtypeStruct((2, 2 * HALF, LANES), BF16)
    wide = pltpu.VMEM((ROWS + 2 * FACE, TILES_WIDE * LANES), BF16)
    weight = pltpu.VMEM((27 * CH, LANES), BF16)
    turned = pltpu.VMEM((CH, ROWS), BF16)
    field, packed = pl.pallas_call(
        functools.partial(section, scale),
        out_shape=(field_shape, packed_shape),
        in_specs=[smem, smem, vmem, vmem, vmem, vmem],
        out_specs=(vmem, vmem),
        scratch_shapes=[
            wide, wide, wide, weight, weight, weight,
            pltpu.VMEM((ROWS, LANES), F32),
            pltpu.VMEM((ROWS, LANES), F32),
            turned, turned,
            *[pltpu.VMEM((2 * FACE, LANES), BF16)] * 4,
            *[pltpu.VMEM((FACE, LANES), BF16)] * 4,
            pltpu.VMEM((2, 2 * HALF, LANES), F32),
            pltpu.VMEM((2, HALF, LANES), F32),
            pltpu.VMEM((2, 8, PART, LANES), BF16),
            pltpu.VMEM((2, 8, PART, LANES), BF16),
            pltpu.VMEM((2, PART, LANES), F32),
            pltpu.VMEM((2, 8, SHARD, LANES), F32),
            pltpu.VMEM((2, SIZE_X, SHARD, LANES), F32),
            dma((4,)), dma((4,)),
            *[dma((2, 8))] * 6, *[dma((2, 4))] * 2, *[dma((2, 8))] * 6,
        ],
        compiler_params=pltpu.CompilerParams(
            collective_id=0, has_side_effects=True, vmem_limit_bytes=48 * 2**20
        ),
        name="section",
    )(down_list, up_list, voxels[0], cotangent[0], weight_first, weight_second)
    step_rows = TILES_WIDE * CH
    first, second, out_field = pl.pallas_call(
        unpack,
        grid=(3,),
        out_shape=(jax.ShapeDtypeStruct((27 * CH, CH), F32),) * 2 + (field_shape,),
        in_specs=[
            pl.BlockSpec((2, step_rows, LANES), lambda i: (0, i, 0)),
            pl.BlockSpec(field_shape.shape, lambda i: (0, 0, 0, 0, 0)),
        ],
        out_specs=(
            pl.BlockSpec((WIDE, CH), lambda i: (i, 0)),
            pl.BlockSpec((WIDE, CH), lambda i: (i, 0)),
            pl.BlockSpec(field_shape.shape, lambda i: (0, 0, 0, 0, 0)),
        ),
        compiler_params=pltpu.CompilerParams(vmem_limit_bytes=32 * 2**20),
        name="unpack",
    )(packed, field)
    shape = weight_first.shape
    return (out_field[None], first.reshape(shape), second.reshape(shape))


def solution(mesh):
    in_specs = (
        P("rep", "space", None, None, None, None),
        P("rep", "space", None, None, None, None),
        P(),
        P(),
        P("rep", "space"),
        P("rep", "space"),
        P("rep", "space"),
        P("rep", "space", None),
    )
    out_specs = (P("rep", "space", None, None, None, None), P(), P())
    return jax.shard_map(
        on_device, mesh=mesh, in_specs=in_specs, out_specs=out_specs, check_vma=False
    )
```

time: 457 us -> 69.3 us (0.15)
  waiting for transfers between devices: 288 us -> 0 us
  local copies, waits for them, and re-layouts: 70.7 us -> 4.07 us
  Pallas kernels: 0 us -> 63 us
  other arithmetic: 34.9 us -> 0 us
  matrix products: 24.7 us -> 0 us
  starting transfers between devices: 18.5 us -> 0 us
  between operations: 17.8 us -> 1.94 us
    psum x1 -> x0, waiting for transfers between devices: 288 us -> none  [on_device(): first, second = lax.psum((first, second), ('space', 'rep'))]
    pallas_call x0 -> x2, Pallas kernels: none -> 63 us  [the longest x1 60.4 us: on_device(): pl.pallas_call(functools.partial(section, scale), out_shape=(field_shape,...]
    dot_general x45 -> x0, matrix products: 24.7 us -> none  [the longest x27 12.9 us: convolve(): jnp.dot(depth_rows(padded, offset_x, offset_y), stacked, preferred_elemen...]
    gather x27 -> x0, local copies, waits for them, and re-layouts: 20.2 us -> none  [assemble(): jnp.take(sources, links[:, (step_x + 1) * 3 + step_y + 1], axis=0)]
    ppermute x6 -> x0, starting transfers between devices: 18.5 us -> none  [from_behind(): return lax.ppermute(block, axis, route)]
    concatenate x31 -> x0, other arithmetic: 17.5 us -> none  [the longest x21 15.6 us: depth_rows(): jnp.concatenate([slab[:, :, :, depth:depth + brick_edge] for depth in ran...]
    reshape x9 -> x0, local copies, waits for them, and re-layouts: 15.4 us -> none  [depth_rows(): return joined.reshape(-1, 3 * width_in)]
    slice x20 -> x0, local copies, waits for them, and re-layouts: 12.4 us -> none  [the longest x9 8.23 us: depth_rows(): slab[:, :, :, depth:depth + brick_edge]]
  transfers between devices with their start and end apart: 7 -> 0, of which waited for: 2 -> 0; matrix products, arithmetic and copies ran while one was open for 8% -> 0% of each run, Pallas kernels for 0% -> 0%
where the time goes in v1:
time: 69.3 us; the launch traced here: 69 us
  Pallas kernels  63 us (91%)
  local copies, waits for them, and re-layouts  4.07 us (6%)
  between operations  1.94 us (3%)
    pallas_call x1, Pallas kernels, on_device(): pl.pallas_call(functools.partial(section, scale), out_shape=(field_shape,...  60.4 us
    unnamed x8, local copies, waits for them, and re-layouts  4.07 us
    pallas_call x1, Pallas kernels, on_device(): pl.pallas_call(unpack, grid=(3,), out_shape=(jax.ShapeDtypeStruct((27 * C...  2.56 us

profile of v1, /device:TPU:1, one launch (start us, length us, event | category | flops | bytes accessed | tf_op | source)
XLA Modules:
  0.0 69.0 jit_solution(8709805670655432259)
XLA Ops:
  1.9 0.0 copy-start
  1.9 1.1 %copy-done = bf16[27,96,96]{2,1,0:T(8,128)(2,1)S(1)} copy-done((bf16[27,96,96]{2,1,0:T(8,128)(2,1)S(1)}, bf16[27,96,96]{2,1,0:T(8,128)(2,1)}, u32[]{:S(2)}) %copy-start) | copy-done | bytes 497688
  3.0 0.0 copy-start.1
  3.0 1.1 %copy-done.1 = bf16[27,96,96]{2,1,0:T(8,128)(2,1)S(1)} copy-done((bf16[27,96,96]{2,1,0:T(8,128)(2,1)S(1)}, bf16[27,96,96]{2,1,0:T(8,128)(2,1)}, u32[]{:S(2)}) %copy-start.1) | copy-done | bytes 497688
  4.1 0.0 copy-start.2
  4.1 0.9 %copy-done.2 = bf16[1,2,8,8,8,96]{5,4,3,2,1,0:T(8,128)(2,1)S(1)} copy-done((bf16[1,2,8,8,8,96]{5,4,3,2,1,0:T(8,128)(2,1)S(1)}, bf16[1,2,8,8,8,96]{5,4,3,2,1,0:T(8,128)(2,1)}, u32[]{:S(2)}) %copy-start.2) | copy-done | bytes 196632
  5.1 0.0 copy-start.3
  5.1 0.9 %copy-done.3 = bf16[1,2,8,8,8,96]{5,4,3,2,1,0:T(8,128)(2,1)S(1)} copy-done((bf16[1,2,8,8,8,96]{5,4,3,2,1,0:T(8,128)(2,1)S(1)}, bf16[1,2,8,8,8,96]{5,4,3,2,1,0:T(8,128)(2,1)}, u32[]{:S(2)}) %copy-start.3) | copy-done | bytes 196632
  6.0 60.4 %section.1 = (bf16[2,8,8,8,96]{4,3,2,1,0:T(8,128)(2,1)S(1)}, bf16[2,2048,128]{2,1,0:T(8,128)(2,1)S(1)}) custom-call(s32[1,1]{1,0:T(1,128)S(6)} %copy.10.down_ref, s32[1,1]{1,0:T(1,128)S(6)} %copy.9.up_ref, bf16[2,8,8,8,96]{4,3,2,1,0:T(8,128)(2,1)S(1)} %bitcast.5, bf16[2,8,8,8,96]{4,3,2,1,0:T(8,128)(2,1)S(1)} %bitcast.6, bf16[27,96,96]{2,1,0:T(8,128)(2,1)S(1)} %copy-done, ...), custom_call_target="tpu_custom_call" | custom-call | tf_op jit(solution)/shard_map/section/pallas_call | solution.py:402
  66.4 2.6 %unpack.1 = (f32[2592,96]{1,0:T(8,128)}, f32[2592,96]{1,0:T(8,128)}, bf16[2,8,8,8,96]{4,3,2,1,0:T(8,128)(2,1)}) custom-call(bf16[2,2048,128]{2,1,0:T(8,128)(2,1)S(1)} %get-tuple-element.8.packed, bf16[2,8,8,8,96]{4,3,2,1,0:T(8,128)(2,1)S(1)} %get-tuple-element.9.field), custom_call_target="tpu_custom_call" | custom-call | tf_op jit(solution)/shard_map/unpack/pallas_call | solution.py:430
Async XLA Ops:
  1.9 1.1 %copy-start = (bf16[27,96,96]{2,1,0:T(8,128)(2,1)S(1)}, bf16[27,96,96]{2,1,0:T(8,128)(2,1)}, u32[]{:S(2)}) copy-start(bf16[27,96,96]{2,1,0:T(8,128)(2,1)} %w1.1) | copy-start | bytes 1492996
  3.0 1.1 %copy-start.1 = (bf16[27,96,96]{2,1,0:T(8,128)(2,1)S(1)}, bf16[27,96,96]{2,1,0:T(8,128)(2,1)}, u32[]{:S(2)}) copy-start(bf16[27,96,96]{2,1,0:T(8,128)(2,1)} %w2.1) | copy-start | bytes 1492996
  4.1 0.9 %copy-start.2 = (bf16[1,2,8,8,8,96]{5,4,3,2,1,0:T(8,128)(2,1)S(1)}, bf16[1,2,8,8,8,96]{5,4,3,2,1,0:T(8,128)(2,1)}, u32[]{:S(2)}) copy-start(bf16[1,2,8,8,8,96]{5,4,3,2,1,0:T(8,128)(2,1)} %param.8) | copy-start | bytes 589828
  5.1 0.9 %copy-start.3 = (bf16[1,2,8,8,8,96]{5,4,3,2,1,0:T(8,128)(2,1)S(1)}, bf16[1,2,8,8,8,96]{5,4,3,2,1,0:T(8,128)(2,1)}, u32[]{:S(2)}) copy-start(bf16[1,2,8,8,8,96]{5,4,3,2,1,0:T(8,128)(2,1)} %param.9) | copy-start | bytes 589828

commit v2 on v1

--- a/solution.py
+++ b/solution.py
@@ -22,8 +22,10 @@
 WIDE = 9 * CH
 TILES_WIDE = 7
 HALF = 1024
-PART = 128
-SHARD = 16
+RINGS = ((SIZE_Y, SIZE_Z, SIZE_X), (SIZE_X, SIZE_Y, SIZE_Z))
+PART = tuple(HALF // ring[0] for ring in RINGS)
+SHARD = tuple(HALF // (ring[0] * ring[1]) for ring in RINGS)
+ORDER = {8: (4, 3, 5, 2, 6, 1, 7), 4: (2, 1, 3)}
 CHUNK = 4
 STEP = CHUNK * FACE
 
@@ -71,12 +73,13 @@
 
 def section(
     scale,
-    down_ref, up_ref, vox, cot, w1, w2,
+    down_ref, up_ref, vox_hbm, cot_hbm, w1_hbm, w2_hbm,
     out, packed,
-    ax, ah, ag, wa, wb, wt, dslope, sums, st, ct,
+    vox, cot, w1, w2, ax, ah, ag, wt, dslope, sums, st, ct,
     up_send, down_send, from_lo, from_hi, hup_send, hdown_send, hfrom_lo, hfrom_hi,
-    part_sum, core_in, ring_out, ring_in, mid, mid_in, cross,
-    halo_s, halo_r, s0, r0, s1, r1, s2, r2, s3, r3, s4, r4, s5, r5, s6, r6,
+    part_sum, core_in,
+    ring_out0, ring_out1, ring_in0, ring_in1, mid0, mid1, mid_in0, mid_in1, cross0, cross1,
+    load_s, halo_s, halo_r, s0, r0, s1, r1, s2, r2, s3, r3, s4, r4, s5, r5, s6, r6,
 ):
     space = lax.axis_index("space")
     rep = lax.axis_index("rep")
@@ -90,17 +93,17 @@
     def device(x, y, z, c):
         return ((x * SIZE_Z + z) * 2 + lax.rem(y, 2), lax.div(y, 2) * 2 + c)
 
-    pos1 = my_y * (1 - core) + my_z * core
-    pos2 = my_z * (1 - core) + my_y * core
-
-    def ring1(t):
-        return device(my_x, t * (1 - core) + my_y * core, my_z * (1 - core) + t * core, core)
-
-    def ring2(t):
-        return device(my_x, my_y * (1 - core) + t * core, t * (1 - core) + my_z * core, core)
-
-    def across(t):
-        return device(t, my_y, my_z, core)
+    first_yz = (
+        my_y * (1 - core) + my_z * core,
+        lambda t: device(my_x, t * (1 - core) + my_y * core, my_z * (1 - core) + t * core, core),
+    )
+    second_yz = (
+        my_z * (1 - core) + my_y * core,
+        lambda t: device(my_x, my_y * (1 - core) + t * core, t * (1 - core) + my_z * core, core),
+    )
+    along_x = (my_x, lambda t: device(t, my_y, my_z, core))
+    axes = ((first_yz, second_yz, along_x), (along_x, first_yz, second_yz))
+    twin_place = (second_yz[0], my_x)
 
     twin = device(my_x, my_y, my_z, 1 - core)
     above = (lax.rem(space + 1, owners), rep)
@@ -120,11 +123,19 @@
             device_id=target, device_id_type=MESH,
         ).wait_recv()
 
+    loads = [
+        pltpu.make_async_copy(src, dst, load_s.at[n])
+        for n, (src, dst) in enumerate(
+            ((vox_hbm, vox), (cot_hbm, cot), (w1_hbm, w1), (w2_hbm, w2))
+        )
+    ]
+    for load in loads:
+        load.start()
+
     barrier = pltpu.get_barrier_semaphore()
     partners = [above, below, twin]
-    partners += [ring1(lax.rem(pos1 + d, 8)) for d in range(1, 8)]
-    partners += [ring2(lax.rem(pos2 + d, 8)) for d in range(1, 8)]
-    partners += [across(lax.rem(my_x + d, SIZE_X)) for d in range(1, SIZE_X)]
+    for (place, at), size in zip(axes[0], RINGS[0]):
+        partners += [at(lax.rem(place + d, size)) for d in range(1, size)]
     for partner in partners:
         pl.semaphore_signal(barrier, inc=1, device_id=partner, device_id_type=MESH)
 
@@ -137,6 +148,8 @@
         chosen = jnp.where(slot == 0, first, jnp.where(slot == 1, second, 0.0))
         return chosen.reshape(FACE, LANES).astype(BF16)
 
+    loads[0].wait()
+    loads[1].wait()
     for at, field in enumerate((vox, cot)):
         up_send[at * FACE : (at + 1) * FACE] = face(field, up, EDGE - 1)
         down_send[at * FACE : (at + 1) * FACE] = face(field, down, 0)
@@ -153,20 +166,22 @@
             spread(chosen, wide, pl.multiple_of(FACE + c * STEP, FACE))
             return carry
 
-        lax.fori_loop(0, 4, body, 0)
+        lax.fori_loop(0, 4, body, 0, unroll=True)
 
     fill(vox, ax)
 
-    def weights(o, carry):
-        rows = pl.ds(pl.multiple_of(o * CH, CH), CH)
-        wa[rows] = widen(w1[o]).astype(BF16)
-        own = widen(w2[o])
-        wb[rows] = own.astype(BF16)
-        square = jnp.concatenate([own, jnp.zeros((LANES - CH, LANES), F32)], axis=0)
-        wt[pl.ds(pl.multiple_of((26 - o) * CH, CH), CH)] = square.T[:CH].astype(BF16)
-        return carry
-
-    lax.fori_loop(0, 27, weights, 0)
+    loads[2].wait()
+    loads[3].wait()
+
+    def weights(n, carry):
+        for k in range(3):
+            o = 3 * n + k
+            own = widen(w2[o])
+            square = jnp.concatenate([own, jnp.zeros((LANES - CH, LANES), F32)], axis=0)
+            wt[26 - o] = square.T[:CH, :CH].astype(BF16)
+        return carry
+
+    lax.fori_loop(0, 9, weights, 0, unroll=True)
     fill(cot, ag)
 
     def cot_turn(c, carry):
@@ -174,7 +189,7 @@
         ct[:, pl.ds(pl.multiple_of(c * STEP, STEP), STEP)] = block.astype(F32).T[:CH].astype(BF16)
         return carry
 
-    lax.fori_loop(0, 4, cot_turn, 0)
+    lax.fori_loop(0, 4, cot_turn, 0, unroll=True)
 
     def edge_in(buffer, at, valid, wide, row):
         block = buffer[at * FACE : (at + 1) * FACE].astype(F32)
@@ -196,14 +211,17 @@
         for i in range(3):
             rows = pl.ds(pl.multiple_of(c * STEP + i * FACE, FACE), STEP)
             product = jnp.dot(
-                wide[rows, :WIDE], weight[i * WIDE : (i + 1) * WIDE], preferred_element_type=F32
+                wide[rows, :WIDE],
+                weight[9 * i : 9 * i + 9].reshape(WIDE, CH),
+                preferred_element_type=F32,
             )
             total = product if total is None else total + product
+        total = widen(total)
         active = jnp.where(c < 2, down, up) < 2
         return total, active
 
     def first_conv(c):
-        total, active = convolve(ax, wa, c)
+        total, active = convolve(ax, w1, c)
         before = jnp.where(active, total, 0.0)
         gate = jax.nn.sigmoid(before)
         dslope[pl.ds(pl.multiple_of(c * STEP, STEP), STEP)] = gate * (1.0 + before * (1.0 - gate))
@@ -216,7 +234,7 @@
         first_conv(n * 3)
         return carry
 
-    lax.fori_loop(0, 2, both_ends, 0)
+    lax.fori_loop(0, 2, both_ends, 0, unroll=True)
     centre = slice(3 * LANES, 4 * LANES)
     hdown_send[...] = ah[FACE : 2 * FACE, centre]
     hup_send[...] = ah[ROWS : ROWS + FACE, centre]
@@ -227,7 +245,7 @@
         first_conv(n + 1)
         return carry
 
-    lax.fori_loop(0, 2, middle, 0)
+    lax.fori_loop(0, 2, middle, 0, unroll=True)
 
     def through(c, carry):
         total, active = convolve(ag, wt, c)
@@ -236,7 +254,7 @@
         st[:, rows] = slope.T[:CH].astype(BF16)
         return carry
 
-    lax.fori_loop(0, 4, through, 0)
+    lax.fori_loop(0, 4, through, 0, unroll=True)
 
     def gradient(turned, wide, g):
         def body(i, carry):
@@ -247,99 +265,109 @@
                 part_sum[g, pl.ds(at, CH)] = block[:, LANES * tile : LANES * (tile + 1)]
             return carry
 
-        lax.fori_loop(0, 3, body, 0)
+        lax.fori_loop(0, 3, body, 0, unroll=True)
         used = 3 * TILES_WIDE * CH
         part_sum[g, used:] = jnp.zeros((2 * HALF - used, LANES), F32)
 
+    ring_out = (ring_out0, ring_out1)
+    ring_in = (ring_in0, ring_in1)
+    mid = (mid0, mid1)
+    mid_in = (mid_in0, mid_in1)
+    cross = (cross0, cross1)
+
     def rows_of(start, count):
-        return pl.ds(pl.multiple_of(start, SHARD), count)
+        return pl.ds(pl.multiple_of(start, 16), count)
 
     def core_send(g):
-        for t in range(8):
-            src = part_sum.at[g, rows_of((1 - core) * HALF + t * PART, PART)]
-            sent.append(
-                send(src, core_in.at[g, pl.ds(t * PART, PART)], s0.at[g, t], r0.at[g, t], twin)
-            )
+        part = PART[g]
+        for t in range(RINGS[g][0]):
+            src = part_sum.at[g, rows_of((1 - core) * HALF + t * part, part)]
+            dst = core_in.at[g, pl.ds(t * part, part)]
+            sent.append(send(src, dst, s0.at[g, t], r0.at[g, t], twin))
 
     def core_add(g):
-        for t in range(8):
-            arrived(core_in.at[g, pl.ds(t * PART, PART)], s0.at[g, t], r0.at[g, t], twin)
-        for d in (4, 3, 5, 2, 6, 1, 7, 0):
-            t = lax.rem(pos1 + d, 8)
+        part, size, (place, at) = PART[g], RINGS[g][0], axes[g][0]
+        for t in range(size):
+            arrived(core_in.at[g, pl.ds(t * part, part)], s0.at[g, t], r0.at[g, t], twin)
+        for d in ORDER[size] + (0,):
+            t = lax.rem(place + d, size)
             total = (
-                part_sum[g, rows_of(core * HALF + t * PART, PART)]
-                + core_in[g, rows_of(t * PART, PART)]
+                part_sum[g, rows_of(core * HALF + t * part, part)]
+                + core_in[g, rows_of(t * part, part)]
             )
             if d == 0:
-                mid[g] = total
+                mid[g][...] = total
             else:
-                ring_out[g, d] = total.astype(BF16)
-                sent.append(
-                    send(ring_out.at[g, d], ring_in.at[g, d], s1.at[g, d], r1.at[g, d], ring1(t))
-                )
+                ring_out[g][d] = total.astype(BF16)
+                src, dst = ring_out[g].at[d], ring_in[g].at[d]
+                sent.append(send(src, dst, s1.at[g, d], r1.at[g, d], at(t)))
 
     def ring1_add(g):
-        for d in range(1, 8):
-            arrived(ring_in.at[g, d], s1.at[g, d], r1.at[g, d], twin)
-        total = mid[g]
-        for d in range(1, 8):
-            total = total + ring_in[g, d].astype(F32)
-        mid[g] = total
-        for d in (4, 3, 5, 2, 6, 1, 7):
-            t = lax.rem(pos2 + d, 8)
-            src = mid.at[g, rows_of(t * SHARD, SHARD)]
-            sent.append(send(src, mid_in.at[g, d], s2.at[g, d], r2.at[g, d], ring2(t)))
+        shard, size, (place, at) = SHARD[g], RINGS[g][1], axes[g][1]
+        total = mid[g][...]
+        for d in range(1, RINGS[g][0]):
+            arrived(ring_in[g].at[d], s1.at[g, d], r1.at[g, d], twin)
+            total = total + ring_in[g][d].astype(F32)
+        mid[g][...] = total
+        for d in ORDER[size]:
+            t = lax.rem(place + d, size)
+            src = mid[g].at[rows_of(t * shard, shard)]
+            sent.append(send(src, mid_in[g].at[d], s2.at[g, d], r2.at[g, d], at(t)))
 
     def ring2_add(g):
-        for d in range(1, 8):
-            arrived(mid_in.at[g, d], s2.at[g, d], r2.at[g, d], twin)
-        total = mid[g, rows_of(pos2 * SHARD, SHARD)]
-        for d in range(1, 8):
-            total = total + mid_in[g, d]
-        cross[g, my_x] = total
-        for d in (2, 1, 3):
-            t = lax.rem(my_x + d, SIZE_X)
-            sent.append(
-                send(cross.at[g, my_x], cross.at[g, my_x], s3.at[g, d], r3.at[g, d], across(t))
-            )
+        shard, size, (place, at) = SHARD[g], RINGS[g][2], axes[g][2]
+        total = mid[g][rows_of(axes[g][1][0] * shard, shard)]
+        for d in range(1, RINGS[g][1]):
+            arrived(mid_in[g].at[d], s2.at[g, d], r2.at[g, d], twin)
+            total = total + mid_in[g][d]
+        cross[g][place] = total
+        mine = cross[g].at[place]
+        for d in ORDER[size]:
+            sent.append(send(mine, mine, s3.at[g, d], r3.at[g, d], at(lax.rem(place + d, size))))
+
+    def start_of(g):
+        return core * HALF + axes[g][0][0] * PART[g]
 
     def cross_add(g):
-        for d in range(1, SIZE_X):
-            t = lax.rem(my_x + SIZE_X - d, SIZE_X)
-            arrived(cross.at[g, t], s3.at[g, d], r3.at[g, d], twin)
-        total = cross[g, 0]
-        for t in range(1, SIZE_X):
-            total = total + cross[g, t]
-        mine = rows_of(core * HALF + pos1 * PART + pos2 * SHARD, SHARD)
-        packed[g, mine] = (total * scale).astype(BF16)
-        for d in (4, 3, 5, 2, 6, 1, 7):
-            t = lax.rem(pos2 + d, 8)
-            sent.append(
-                send(packed.at[g, mine], packed.at[g, mine], s4.at[g, d], r4.at[g, d], ring2(t))
-            )
+        size, place = RINGS[g][2], axes[g][2][0]
+        for d in range(1, size):
+            t = lax.rem(place + size - d, size)
+            arrived(cross[g].at[t], s3.at[g, d], r3.at[g, d], twin)
+        total = cross[g][0]
+        for t in range(1, size):
+            total = total + cross[g][t]
+        shard, size, (place, at) = SHARD[g], RINGS[g][1], axes[g][1]
+        rows = rows_of(start_of(g) + place * shard, shard)
+        packed[g, rows] = (total * scale).astype(BF16)
+        mine = packed.at[g, rows]
+        for d in ORDER[size]:
+            sent.append(send(mine, mine, s4.at[g, d], r4.at[g, d], at(lax.rem(place + d, size))))
 
     def ring2_gather(g):
-        for d in range(1, 8):
-            t = lax.rem(pos2 + 8 - d, 8)
-            theirs = rows_of(core * HALF + pos1 * PART + t * SHARD, SHARD)
-            arrived(packed.at[g, theirs], s4.at[g, d], r4.at[g, d], twin)
-        mine = packed.at[g, rows_of(core * HALF + pos1 * PART, PART)]
-        for d in (4, 3, 5, 2, 6, 1, 7):
-            t = lax.rem(pos1 + d, 8)
-            sent.append(send(mine, mine, s5.at[g, d], r5.at[g, d], ring1(t)))
+        shard, size, place = SHARD[g], RINGS[g][1], axes[g][1][0]
+        for d in range(1, size):
+            t = lax.rem(place + size - d, size)
+            theirs = packed.at[g, rows_of(start_of(g) + t * shard, shard)]
+            arrived(theirs, s4.at[g, d], r4.at[g, d], twin)
+        mine = packed.at[g, rows_of(start_of(g), PART[g])]
+        size, (place, at) = RINGS[g][0], axes[g][0]
+        for d in ORDER[size]:
+            sent.append(send(mine, mine, s5.at[g, d], r5.at[g, d], at(lax.rem(place + d, size))))
         sent.append(send(mine, mine, s6.at[g, 0], r6.at[g, 0], twin))
 
     def ring1_gather(g):
-        for d in (1, 7, 2, 6, 3, 5, 4):
-            t = lax.rem(pos1 + 8 - d, 8)
-            theirs = packed.at[g, rows_of(core * HALF + t * PART, PART)]
+        size, place = RINGS[g][0], axes[g][0][0]
+        for d in ORDER[size][::-1]:
+            t = lax.rem(place + size - d, size)
+            theirs = packed.at[g, rows_of(core * HALF + t * PART[g], PART[g])]
             arrived(theirs, s5.at[g, d], r5.at[g, d], twin)
             sent.append(send(theirs, theirs, s6.at[g, d], r6.at[g, d], twin))
 
     def core_gather(g):
-        for d in range(8):
-            t = lax.rem(pos2 + 8 - d, 8)
-            theirs = packed.at[g, rows_of((1 - core) * HALF + t * PART, PART)]
+        size = RINGS[g][0]
+        for d in range(size):
+            t = lax.rem(twin_place[g] + size - d, size)
+            theirs = packed.at[g, rows_of((1 - core) * HALF + t * PART[g], PART[g])]
             arrived(theirs, s6.at[g, d], r6.at[g, d], twin)
 
     gradient(st, ax, 0)
@@ -354,13 +382,13 @@
     core_add(1)
 
     def second_conv(c, carry):
-        total, active = convolve(ah, wb, c)
+        total, active = convolve(ah, w2, c)
         inputs = ax[pl.ds(pl.multiple_of(FACE + c * STEP, FACE), STEP), centre].astype(F32)
         rows = pl.ds(pl.multiple_of(c * STEP, STEP), STEP)
         sums[rows] = jnp.where(active, total + inputs, 0.0)
         return carry
 
-    lax.fori_loop(0, 4, second_conv, 0)
+    lax.fori_loop(0, 4, second_conv, 0, unroll=True)
 
     def place(n, carry):
         low = sums[pl.ds(pl.multiple_of(n * STEP, STEP), STEP)]
@@ -371,7 +399,7 @@
             out[slot, pl.ds(n * CHUNK, CHUNK)] = chosen.astype(BF16)
         return carry
 
-    lax.fori_loop(0, 2, place, 0)
+    lax.fori_loop(0, 2, place, 0, unroll=True)
 
     for stage in (ring1_add, ring2_add, cross_add, ring2_gather, ring1_gather, core_gather):
         for g in range(2):
@@ -397,15 +425,16 @@
     field_shape = jax.ShapeDtypeStruct((2, EDGE, EDGE, EDGE, CH), BF16)
     packed_shape = jax.ShapeDtypeStruct((2, 2 * HALF, LANES), BF16)
     wide = pltpu.VMEM((ROWS + 2 * FACE, TILES_WIDE * LANES), BF16)
-    weight = pltpu.VMEM((27 * CH, LANES), BF16)
+    weight = pltpu.VMEM((27, CH, CH), BF16)
+    bricks = pltpu.VMEM(field_shape.shape, BF16)
     turned = pltpu.VMEM((CH, ROWS), BF16)
     field, packed = pl.pallas_call(
         functools.partial(section, scale),
         out_shape=(field_shape, packed_shape),
-        in_specs=[smem, smem, vmem, vmem, vmem, vmem],
+        in_specs=[smem, smem] + [pl.BlockSpec(memory_space=pltpu.HBM)] * 4,
         out_specs=(vmem, vmem),
         scratch_shapes=[
-            wide, wide, wide, weight, weight, weight,
+            bricks, bricks, weight, weight, wide, wide, wide, weight,
             pltpu.VMEM((ROWS, LANES), F32),
             pltpu.VMEM((ROWS, LANES), F32),
             turned, turned,
@@ -413,19 +442,19 @@
             *[pltpu.VMEM((FACE, LANES), BF16)] * 4,
             pltpu.VMEM((2, 2 * HALF, LANES), F32),
             pltpu.VMEM((2, HALF, LANES), F32),
-            pltpu.VMEM((2, 8, PART, LANES), BF16),
-            pltpu.VMEM((2, 8, PART, LANES), BF16),
-            pltpu.VMEM((2, PART, LANES), F32),
-            pltpu.VMEM((2, 8, SHARD, LANES), F32),
-            pltpu.VMEM((2, SIZE_X, SHARD, LANES), F32),
+            *[pltpu.VMEM((ring[0], part, LANES), BF16) for ring, part in zip(RINGS, PART)] * 2,
+            *[pltpu.VMEM((part, LANES), F32) for part in PART],
+            *[pltpu.VMEM((ring[1], shard, LANES), F32) for ring, shard in zip(RINGS, SHARD)],
+            *[pltpu.VMEM((ring[2], shard, LANES), F32) for ring, shard in zip(RINGS, SHARD)],
+            dma((4,)),
             dma((4,)), dma((4,)),
-            *[dma((2, 8))] * 6, *[dma((2, 4))] * 2, *[dma((2, 8))] * 6,
+            *[dma((2, 8))] * 14,
         ],
         compiler_params=pltpu.CompilerParams(
             collective_id=0, has_side_effects=True, vmem_limit_bytes=48 * 2**20
         ),
         name="section",
-    )(down_list, up_list, voxels[0], cotangent[0], weight_first, weight_second)
+    )(down_list, up_list, *[pltpu.with_memory_space_constraint(a, pltpu.HBM) for a in (voxels[0], cotangent[0], weight_first, weight_second)])
     step_rows = TILES_WIDE * CH
     first, second, out_field = pl.pallas_call(
         unpack,

time: 69.3 us -> 59.5 us (0.86)
  Pallas kernels: 63 us -> 57.4 us
  local copies, waits for them, and re-layouts: 4.07 us -> 0 us
    pallas_call x1, Pallas kernels: 60.4 us -> 54.9 us  [on_device(): pl.pallas_call(functools.partial(section, scale), out_shape=(field_shape,...]
    unnamed x8 -> x0, local copies, waits for them, and re-layouts: 4.07 us -> none
where the time goes in v2:
time: 59.5 us; the launch traced here: 59.3 us
  Pallas kernels  57.4 us (96%)
  between operations  1.93 us (3%)
    pallas_call x1, Pallas kernels, on_device(): pl.pallas_call(functools.partial(section, scale), out_shape=(field_shape,...  54.9 us
    pallas_call x1, Pallas kernels, on_device(): pl.pallas_call(unpack, grid=(3,), out_shape=(jax.ShapeDtypeStruct((27 * C...  2.56 us

profile of v2, /device:TPU:1, one launch (start us, length us, event | category | flops | bytes accessed | tf_op | source)
XLA Modules:
  0.0 59.3 jit_solution(7761302758266445206)
XLA Ops:
  1.9 54.9 %section.1 = (bf16[2,8,8,8,96]{4,3,2,1,0:T(8,128)(2,1)S(1)}, bf16[2,2048,128]{2,1,0:T(8,128)(2,1)S(1)}) custom-call(s32[1,1]{1,0:T(1,128)S(6)} %copy.10.down_ref, s32[1,1]{1,0:T(1,128)S(6)} %copy.9.up_ref, bf16[2,8,8,8,96]{4,3,2,1,0:T(8,128)(2,1)} %bitcast.5, bf16[2,8,8,8,96]{4,3,2,1,0:T(8,128)(2,1)} %bitcast.6, bf16[27,96,96]{2,1,0:T(8,128)(2,1)} %w1_hbm.1, ...), custom_call_target="tpu_custom_call" | custom-call | tf_op jit(solution)/shard_map/section/pallas_call | solution.py:431
  56.8 2.6 %unpack.1 = (f32[2592,96]{1,0:T(8,128)}, f32[2592,96]{1,0:T(8,128)}, bf16[2,8,8,8,96]{4,3,2,1,0:T(8,128)(2,1)}) custom-call(bf16[2,2048,128]{2,1,0:T(8,128)(2,1)S(1)} %get-tuple-element.8.packed, bf16[2,8,8,8,96]{4,3,2,1,0:T(8,128)(2,1)S(1)} %get-tuple-element.9.field), custom_call_target="tpu_custom_call" | custom-call | tf_op jit(solution)/shard_map/unpack/pallas_call | solution.py:459

commit v3 on v2

v3 whole, which is shorter than its diff:
```python
import functools
import math

import jax
import jax.numpy as jnp
from jax import lax
from jax.experimental import pallas as pl
from jax.experimental.pallas import tpu as pltpu
from jax.sharding import PartitionSpec as P

F32 = jnp.float32
BF16 = jnp.bfloat16
MESH = pl.DeviceIdType.MESH

SIZE_X, SIZE_Y, SIZE_Z = 4, 8, 8
EDGE = 8
CH = 96
LANES = 128
FACE = EDGE * EDGE
PLANES = 2 * EDGE
ROWS = PLANES * FACE
WIDE = 9 * CH
TILES_WIDE = 7
HALF = 1024
GROUP = HALF // SIZE_X
SIDE = 8
SHARD = GROUP // SIDE
STEPS_X = (2, 1, 3, 0)
STEPS = (4, 3, 5, 2, 6, 1, 7)
PLANE = tuple((a, b) for a in STEPS_X for b in STEPS + (0,) if a or b)
AHEAD = 2
CHUNK = 4
STEP = CHUNK * FACE


def widen(value):
    value = value.astype(F32)
    blank = jnp.zeros(value.shape[:-1] + (LANES - CH,), F32)
    return jnp.concatenate([value, blank], axis=-1)


def spread(value, out, row):
    planes = value.shape[0]
    flat = value.reshape(planes * EDGE, EDGE, LANES)
    depth = lax.broadcasted_iota(jnp.int32, flat.shape, 1)
    by_depth = [
        jnp.where(depth == 0, 0.0, pltpu.roll(flat, 1, 1)),
        flat,
        jnp.where(depth == EDGE - 1, 0.0, pltpu.roll(flat, EDGE - 1, 1)),
    ]

    def piece(index):
        shift_y, shift_z = index // 3, index % 3
        turned = by_depth[shift_z]
        turn = CH * index % LANES
        if turn:
            turned = pltpu.roll(turned, turn, 2)
        turned = turned.reshape(planes, EDGE, EDGE, LANES)
        blank = jnp.zeros((planes, 1, EDGE, LANES), F32)
        if shift_y == 0:
            turned = jnp.concatenate([blank, turned[:, : EDGE - 1]], axis=1)
        elif shift_y == 2:
            turned = jnp.concatenate([turned[:, 1:], blank], axis=1)
        return turned.reshape(planes * FACE, LANES)

    lane = lax.broadcasted_iota(jnp.int32, (planes * FACE, LANES), 1)
    pieces = [piece(index) for index in range(9)]
    for tile in range(TILES_WIDE):
        first = LANES * tile // CH
        border = CH * (first + 1) - LANES * tile
        block = pieces[first]
        if border < LANES and first + 1 < 9:
            block = jnp.where(lane < border, block, pieces[first + 1])
        out[pl.ds(row, planes * FACE), LANES * tile : LANES * (tile + 1)] = block.astype(BF16)


def section(
    scale,
    down_ref, up_ref, table, vox_hbm, cot_hbm, w1_hbm, w2_hbm,
    out, packed,
    vox, cot, w1, w2, ax, ah, ag, wt, dslope, sums, st, ct,
    up_send, down_send, from_lo, from_hi,
    part_sum, core_in, plane_out, plane_in, mid, cross,
    load_s, halo_s, halo_r, s0, r0, s1, r1, s2, r2, s3, r3, s4, r4,
):
    space = lax.axis_index("space")
    rep = lax.axis_index("rep")
    owners = SIZE_X * SIZE_Z * 2
    y_lo = lax.rem(space, 2)
    my_z = lax.rem(lax.div(space, 2), SIZE_Z)
    my_x = lax.div(space, 2 * SIZE_Z)
    core = lax.rem(rep, 2)
    my_y = lax.div(rep, 2) * 2 + y_lo

    def device(x, y, z, c):
        return ((x * SIZE_Z + z) * 2 + lax.rem(y, 2), lax.div(y, 2) * 2 + c)

    side = my_z * (1 - core) + my_y * core
    line = my_y * (1 - core) + my_z * core

    def in_plane(x, t):
        return device(x, my_y * (1 - core) + t * core, t * (1 - core) + my_z * core, core)

    def in_line(t):
        return device(my_x, t * (1 - core) + my_y * core, my_z * (1 - core) + t * core, core)

    def moved(a, b):
        return lax.rem(my_x + a, SIZE_X), lax.rem(side + b, SIDE)

    twin = device(my_x, my_y, my_z, 1 - core)
    above = (lax.rem(space + 1, owners), rep)
    below = (lax.rem(space + owners - 1, owners), rep)

    def send(src, dst, send_sem, recv_sem, target):
        copy = pltpu.make_async_remote_copy(
            src_ref=src, dst_ref=dst, send_sem=send_sem, recv_sem=recv_sem,
            device_id=target, device_id_type=MESH,
        )
        copy.start()
        return copy

    def arrived(dst, send_sem, recv_sem, target):
        pltpu.make_async_remote_copy(
            src_ref=dst, dst_ref=dst, send_sem=send_sem, recv_sem=recv_sem,
            device_id=target, device_id_type=MESH,
        ).wait_recv()

    loads = [
        pltpu.make_async_copy(src, dst, load_s.at[n])
        for n, (src, dst) in enumerate(
            ((vox_hbm, vox), (cot_hbm, cot), (w1_hbm, w1), (w2_hbm, w2))
        )
    ]
    for load in loads:
        load.start()

    barrier = pltpu.get_barrier_semaphore()
    partners = [above, below, twin]
    partners += [in_plane(*moved(a, b)) for a, b in PLANE]
    partners += [in_line(lax.rem(line + d, SIDE)) for d in STEPS]
    for partner in partners:
        pl.semaphore_signal(barrier, inc=1, device_id=partner, device_id_type=MESH)

    down = down_ref[0, 0]
    up = up_ref[0, 0]
    sent = []

    def face(field, slot, plane):
        first, second = widen(field[0, plane]), widen(field[1, plane])
        chosen = jnp.where(slot == 0, first, jnp.where(slot == 1, second, 0.0))
        return chosen.reshape(FACE, LANES).astype(BF16)

    loads[0].wait()
    loads[1].wait()
    faces = ((vox, EDGE - 2, 0), (vox, EDGE - 1, 1), (cot, EDGE - 1, 0))
    for at, (field, high, low) in enumerate(faces):
        up_send[at * FACE : (at + 1) * FACE] = face(field, up, high)
        down_send[at * FACE : (at + 1) * FACE] = face(field, down, low)
    pl.semaphore_wait(barrier, len(partners))
    sent.append(send(up_send, from_lo, halo_s.at[0], halo_r.at[0], above))
    sent.append(send(down_send, from_hi, halo_s.at[1], halo_r.at[1], below))

    def fill(field, wide, ahead):
        def body(c, carry):
            planes = pl.ds(lax.rem(c, 2) * CHUNK, CHUNK)
            slot = jnp.where(c < 2, down, up)
            first, second = widen(field[0, planes]), widen(field[1, planes])
            chosen = jnp.where(slot == 0, first, jnp.where(slot == 1, second, 0.0))
            spread(chosen, wide, pl.multiple_of(ahead * FACE + c * STEP, FACE))
            return carry

        lax.fori_loop(0, 4, body, 0, unroll=True)

    fill(vox, ax, AHEAD)

    loads[2].wait()
    loads[3].wait()

    def weights(n, carry):
        for k in range(3):
            o = 3 * n + k
            own = widen(w2[o])
            square = jnp.concatenate([own, jnp.zeros((LANES - CH, LANES), F32)], axis=0)
            wt[26 - o] = square.T[:CH, :CH].astype(BF16)
        return carry

    lax.fori_loop(0, 9, weights, 0, unroll=True)
    fill(cot, ag, 1)

    def cot_turn(c, carry):
        block = ag[pl.ds(pl.multiple_of(FACE + c * STEP, FACE), STEP), 3 * LANES : 4 * LANES]
        ct[:, pl.ds(pl.multiple_of(c * STEP, STEP), STEP)] = block.astype(F32).T[:CH].astype(BF16)
        return carry

    lax.fori_loop(0, 4, cot_turn, 0, unroll=True)

    def linked(slot, way):
        entry = jnp.where(slot == 0, table[0, 0, way], jnp.where(slot == 1, table[0, 1, way], 3))
        return entry == 2

    lower_active, upper_active = linked(down, 1), linked(up, 7)

    def keep(value, planes):
        kept = []
        for k, plane in enumerate(planes):
            if plane < 0:
                active = lower_active
            elif plane >= PLANES:
                active = upper_active
            else:
                active = (down if plane < EDGE else up) < 2
            kept.append(jnp.where(active, value[k * FACE : (k + 1) * FACE], 0.0))
        return jnp.concatenate(kept, axis=0)

    def runs(planes):
        found = []
        for k, plane in enumerate(planes):
            if k and plane == planes[k - 1] + 1:
                found[-1][2] += 1
            else:
                found.append([k, plane, 1])
        return found

    def convolve(wide, weight, planes, ahead):
        total = None
        for i in range(3):
            rows = [
                wide[(first + ahead - 1 + i) * FACE : (first + ahead - 1 + i + count) * FACE, :WIDE]
                for _, first, count in runs(planes)
            ]
            product = jnp.dot(
                rows[0] if len(rows) == 1 else jnp.concatenate(rows, axis=0),
                weight[9 * i : 9 * i + 9].reshape(WIDE, CH),
                preferred_element_type=F32,
            )
            total = product if total is None else total + product
        return widen(total)

    def first_conv(planes):
        before = keep(convolve(ax, w1, planes, AHEAD), planes)
        gate = jax.nn.sigmoid(before)
        factor = gate * (1.0 + before * (1.0 - gate))
        hidden = (before * gate).astype(BF16).astype(F32)
        for k, plane in enumerate(planes):
            if 0 <= plane < PLANES:
                dslope[plane * FACE : (plane + 1) * FACE] = factor[k * FACE : (k + 1) * FACE]
        for k, first, count in runs(planes):
            block = hidden[k * FACE : (k + count) * FACE].reshape(count, EDGE, EDGE, LANES)
            spread(block, ah, (first + 1) * FACE)

    def through(planes):
        total = keep(convolve(ag, wt, planes, 1), planes)
        for k, first, count in runs(planes):
            rows = slice(first * FACE, (first + count) * FACE)
            slope = total[k * FACE : (k + count) * FACE] * dslope[rows]
            st[:, rows] = slope.T[:CH].astype(BF16)

    inner = ((2, 3, 4, 5), (6, 7, 8, 9), (10, 11, 12, 13))
    for planes in inner:
        first_conv(planes)
    for planes in inner:
        through(planes)

    def edge_in(buffer, at, count, valid, wide, row):
        block = buffer[at * FACE : (at + count) * FACE].astype(F32)
        block = jnp.where(valid, block, 0.0).reshape(count, EDGE, EDGE, LANES)
        spread(block, wide, row)

    lower_valid = space > 0
    upper_valid = space < owners - 1
    arrived(from_lo, halo_s.at[0], halo_r.at[0], above)
    edge_in(from_lo, 0, AHEAD, lower_valid, ax, 0)
    edge_in(from_lo, AHEAD, 1, lower_valid, ag, 0)
    arrived(from_hi, halo_s.at[1], halo_r.at[1], below)
    edge_in(from_hi, 0, AHEAD, upper_valid, ax, (PLANES + AHEAD) * FACE)
    edge_in(from_hi, AHEAD, 1, upper_valid, ag, (PLANES + 1) * FACE)
    first_conv((-1, 0, 1, 14, 15, 16))
    through((0, 1, 14, 15))
    centre = slice(3 * LANES, 4 * LANES)

    def gradient(turned, wide, g, ahead, k):
        i = k * core + (2 - k) * (1 - core)
        rows = pl.ds(pl.multiple_of((i + ahead - 1) * FACE, FACE), ROWS)
        block = jnp.dot(turned[...], wide[rows], preferred_element_type=F32)
        for tile in range(TILES_WIDE):
            at = pl.multiple_of((i * TILES_WIDE + tile) * CH, CH)
            part_sum[g, pl.ds(at, CH)] = block[:, LANES * tile : LANES * (tile + 1)]

    def rows_of(start, count):
        return pl.ds(pl.multiple_of(start, SHARD), count)

    def core_send(g):
        for a in STEPS_X:
            start = lax.rem(my_x + a, SIZE_X) * GROUP
            src = part_sum.at[g, rows_of((1 - core) * HALF + start, GROUP)]
            dst = core_in.at[g, rows_of(start, GROUP)]
            sent.append(send(src, dst, s0.at[g, a], r0.at[g, a], twin))

    def core_add(g):
        for a in STEPS_X:
            start = lax.rem(my_x + a, SIZE_X) * GROUP
            arrived(core_in.at[g, rows_of(start, GROUP)], s0.at[g, a], r0.at[g, a], twin)
            for b in STEPS + (0,):
                x, t = moved(a, b)
                at = x * GROUP + t * SHARD
                total = part_sum[g, rows_of(core * HALF + at, SHARD)] + core_in[g, rows_of(at, SHARD)]
                if (a, b) == (0, 0):
                    mid[g] = total
                else:
                    n = a * SIDE + b
                    plane_out[g, n] = total.astype(BF16)
                    src, dst = plane_out.at[g, n], plane_in.at[g, n]
                    sent.append(send(src, dst, s1.at[g, n], r1.at[g, n], in_plane(x, t)))

    def plane_add(g):
        total = mid[g]
        for a, b in PLANE[::-1]:
            n = a * SIDE + b
            arrived(plane_in.at[g, n], s1.at[g, n], r1.at[g, n], twin)
            total = total + plane_in[g, n].astype(F32)
        cross[g, line] = total
        mine = cross.at[g, line]
        for d in STEPS:
            target = in_line(lax.rem(line + d, SIDE))
            sent.append(send(mine, mine, s2.at[g, d], r2.at[g, d], target))

    def place_of(x, t):
        return rows_of(core * HALF + x * GROUP + t * SHARD, SHARD)

    def line_add(g):
        for d in STEPS[::-1]:
            theirs = cross.at[g, lax.rem(line + SIDE - d, SIDE)]
            arrived(theirs, s2.at[g, d], r2.at[g, d], twin)
        total = cross[g, 0]
        for t in range(1, SIDE):
            total = total + cross[g, t]
        packed[g, place_of(my_x, side)] = (total * scale).astype(BF16)
        mine = packed.at[g, place_of(my_x, side)]
        for a, b in PLANE:
            n = a * SIDE + b
            sent.append(send(mine, mine, s3.at[g, n], r3.at[g, n], in_plane(*moved(a, b))))

    def plane_gather(g):
        for a in STEPS_X[::-1]:
            x = lax.rem(my_x + SIZE_X - a, SIZE_X)
            for b in (0,) + STEPS[::-1]:
                if (a, b) != (0, 0):
                    n = a * SIDE + b
                    theirs = packed.at[g, place_of(x, lax.rem(side + SIDE - b, SIDE))]
                    arrived(theirs, s3.at[g, n], r3.at[g, n], twin)
            group = packed.at[g, rows_of(core * HALF + x * GROUP, GROUP)]
            sent.append(send(group, group, s4.at[g, a], r4.at[g, a], twin))

    def core_gather(g):
        for a in STEPS_X[::-1]:
            x = lax.rem(my_x + SIZE_X - a, SIZE_X)
            group = packed.at[g, rows_of((1 - core) * HALF + x * GROUP, GROUP)]
            arrived(group, s4.at[g, a], r4.at[g, a], twin)

    used = 3 * TILES_WIDE * CH
    for g in range(2):
        part_sum[g, used:] = jnp.zeros((2 * HALF - used, LANES), F32)
    gradient(st, ax, 0, AHEAD, 0)
    gradient(st, ax, 0, AHEAD, 1)
    core_send(0)
    gradient(st, ax, 0, AHEAD, 2)
    gradient(ct, ah, 1, 1, 0)
    gradient(ct, ah, 1, 1, 1)
    core_send(1)
    core_add(0)
    gradient(ct, ah, 1, 1, 2)
    core_add(1)

    for planes in ((0, 1, 2, 3), (4, 5, 6, 7), (8, 9, 10, 11), (12, 13, 14, 15)):
        first, count = planes[0], len(planes)
        total = convolve(ah, w2, planes, 1)
        inputs = ax[(first + AHEAD) * FACE : (first + AHEAD + count) * FACE, centre].astype(F32)
        sums[first * FACE : (first + count) * FACE] = keep(total + inputs, planes)

    def place(n, carry):
        low = sums[pl.ds(pl.multiple_of(n * STEP, STEP), STEP)]
        high = sums[pl.ds(pl.multiple_of(ROWS // 2 + n * STEP, STEP), STEP)]
        for slot in range(2):
            chosen = jnp.where(down == slot, low, jnp.where(up == slot, high, 0.0))
            chosen = chosen.reshape(CHUNK, EDGE, EDGE, LANES)[..., :CH]
            out[slot, pl.ds(n * CHUNK, CHUNK)] = chosen.astype(BF16)
        return carry

    lax.fori_loop(0, 2, place, 0, unroll=True)

    for stage in (plane_add, line_add, plane_gather, core_gather):
        for g in range(2):
            stage(g)
    for copy in sent:
        copy.wait_send()


def unpack(packed, field, first, second, out):
    out[...] = field[...]
    for g, result in enumerate((first, second)):
        for tile in range(TILES_WIDE):
            turned = packed[g, CH * tile : CH * (tile + 1)].astype(F32).T
            count = min(LANES, WIDE - LANES * tile)
            result[LANES * tile : LANES * tile + count] = turned[:count]


def on_device(voxels, cotangent, weight_first, weight_second, act_count, up_list, down_list, table):
    vmem = pl.BlockSpec(memory_space=pltpu.VMEM)
    smem = pl.BlockSpec(memory_space=pltpu.SMEM)
    scale = 1.0 / math.sqrt(512 * 2 * EDGE**3)
    dma = pltpu.SemaphoreType.DMA
    field_shape = jax.ShapeDtypeStruct((2, EDGE, EDGE, EDGE, CH), BF16)
    packed_shape = jax.ShapeDtypeStruct((2, 2 * HALF, LANES), BF16)
    wide = pltpu.VMEM((ROWS + 2 * FACE, TILES_WIDE * LANES), BF16)
    wider = pltpu.VMEM((ROWS + 2 * AHEAD * FACE, TILES_WIDE * LANES), BF16)
    weight = pltpu.VMEM((27, CH, CH), BF16)
    bricks = pltpu.VMEM(field_shape.shape, BF16)
    turned = pltpu.VMEM((CH, ROWS), BF16)
    field, packed = pl.pallas_call(
        functools.partial(section, scale),
        out_shape=(field_shape, packed_shape),
        in_specs=[smem, smem, smem] + [pl.BlockSpec(memory_space=pltpu.HBM)] * 4,
        out_specs=(vmem, vmem),
        scratch_shapes=[
            bricks, bricks, weight, weight, wider, wide, wide, weight,
            pltpu.VMEM((ROWS, LANES), F32),
            pltpu.VMEM((ROWS, LANES), F32),
            turned, turned,
            *[pltpu.VMEM(((AHEAD + 1) * FACE, LANES), BF16)] * 4,
            pltpu.VMEM((2, 2 * HALF, LANES), F32),
            pltpu.VMEM((2, HALF, LANES), F32),
            pltpu.VMEM((2, SIZE_X * SIDE, SHARD, LANES), BF16),
            pltpu.VMEM((2, SIZE_X * SIDE, SHARD, LANES), BF16),
            pltpu.VMEM((2, SHARD, LANES), F32),
            pltpu.VMEM((2, SIDE, SHARD, LANES), F32),
            dma((4,)), dma((2,)), dma((2,)),
            *[dma((2, SIZE_X))] * 2, *[dma((2, SIZE_X * SIDE))] * 2,
            *[dma((2, SIDE))] * 2, *[dma((2, SIZE_X * SIDE))] * 2, *[dma((2, SIZE_X))] * 2,
        ],
        compiler_params=pltpu.CompilerParams(
            collective_id=0, has_side_effects=True, vmem_limit_bytes=48 * 2**20
        ),
        name="section",
    )(
        down_list, up_list, table,
        *[
            pltpu.with_memory_space_constraint(array, pltpu.HBM)
            for array in (voxels[0], cotangent[0], weight_first, weight_second)
        ],
    )
    step_rows = TILES_WIDE * CH
    first, second, out_field = pl.pallas_call(
        unpack,
        grid=(3,),
        out_shape=(jax.ShapeDtypeStruct((27 * CH, CH), F32),) * 2 + (field_shape,),
        in_specs=[
            pl.BlockSpec((2, step_rows, LANES), lambda i: (0, i, 0)),
            pl.BlockSpec(field_shape.shape, lambda i: (0, 0, 0, 0, 0)),
        ],
        out_specs=(
            pl.BlockSpec((WIDE, CH), lambda i: (i, 0)),
            pl.BlockSpec((WIDE, CH), lambda i: (i, 0)),
            pl.BlockSpec(field_shape.shape, lambda i: (0, 0, 0, 0, 0)),
        ),
        compiler_params=pltpu.CompilerParams(vmem_limit_bytes=32 * 2**20),
        name="unpack",
    )(packed, field)
    shape = weight_first.shape
    return (out_field[None], first.reshape(shape), second.reshape(shape))


def solution(mesh):
    in_specs = (
        P("rep", "space", None, None, None, None),
        P("rep", "space", None, None, None, None),
        P(),
        P(),
        P("rep", "space"),
        P("rep", "space"),
        P("rep", "space"),
        P("rep", "space", None),
    )
    out_specs = (P("rep", "space", None, None, None, None), P(), P())
    return jax.shard_map(
        on_device, mesh=mesh, in_specs=in_specs, out_specs=out_specs, check_vma=False
    )
```

time: 59.5 us -> 57.9 us (0.973)
  Pallas kernels: 57.4 us -> 55.1 us
  local copies, waits for them, and re-layouts: 0 us -> 0.67 us
    pallas_call x1, Pallas kernels: 54.9 us -> 52.5 us  [on_device(): pl.pallas_call(functools.partial(section, scale), out_shape=(field_shape,...]
    unnamed x0 -> x2, local copies, waits for them, and re-layouts: none -> 0.67 us
where the time goes in v3:
time: 57.9 us; the launch traced here: 57.7 us
  Pallas kernels  55.1 us (95%)
  between operations  1.94 us (3%)
  local copies, waits for them, and re-layouts  0.67 us (1%)
    pallas_call x1, Pallas kernels, on_device(): pl.pallas_call(functools.partial(section, scale), out_shape=(field_shape,...  52.5 us
    pallas_call x1, Pallas kernels, on_device(): pl.pallas_call(unpack, grid=(3,), out_shape=(jax.ShapeDtypeStruct((27 * C...  2.56 us

profile of v3, /device:TPU:1, one launch (start us, length us, event | category | flops | bytes accessed | tf_op | source)
XLA Modules:
  0.0 57.7 jit_solution(5384374612956836847)
XLA Ops:
  1.9 0.0 copy-start
  1.9 0.7 %copy-done = s32[1,2,9]{2,1,0:T(2,128)S(1)} copy-done((s32[1,2,9]{2,1,0:T(2,128)S(1)}, s32[1,2,9]{2,1,0:T(2,128)}, u32[]{:S(2)}) %copy-start) | copy-done | bytes 96
  2.6 52.5 %section.1 = (bf16[2,8,8,8,96]{4,3,2,1,0:T(8,128)(2,1)S(1)}, bf16[2,2048,128]{2,1,0:T(8,128)(2,1)S(1)}) custom-call(s32[1,1]{1,0:T(1,128)S(6)} %copy.11.down_ref, s32[1,1]{1,0:T(1,128)S(6)} %copy.10.up_ref, s32[1,2,9]{2,1,0:T(2,128)S(1)} %copy-done, bf16[2,8,8,8,96]{4,3,2,1,0:T(8,128)(2,1)} %bitcast.5, bf16[2,8,8,8,96]{4,3,2,1,0:T(8,128)(2,1)} %bitcast.6, ...), custom_call_target="tpu_custom_call" | custom-call | tf_op jit(solution)/shard_map/section/pallas_call | solution.py:419
  55.1 2.6 %unpack.1 = (f32[2592,96]{1,0:T(8,128)}, f32[2592,96]{1,0:T(8,128)}, bf16[2,8,8,8,96]{4,3,2,1,0:T(8,128)(2,1)}) custom-call(bf16[2,2048,128]{2,1,0:T(8,128)(2,1)S(1)} %get-tuple-element.8.packed, bf16[2,8,8,8,96]{4,3,2,1,0:T(8,128)(2,1)S(1)} %get-tuple-element.9.field), custom_call_target="tpu_custom_call" | custom-call | tf_op jit(solution)/shard_map/unpack/pallas_call | solution.py:452
Async XLA Ops:
  1.9 0.7 %copy-start = (s32[1,2,9]{2,1,0:T(2,128)S(1)}, s32[1,2,9]{2,1,0:T(2,128)}, u32[]{:S(2)}) copy-start(s32[1,2,9]{2,1,0:T(2,128)} %table.1) | copy-start | bytes 220

commit v4 on v3

--- a/solution.py
+++ b/solution.py
@@ -28,6 +28,7 @@
 STEPS_X = (2, 1, 3, 0)
 STEPS = (4, 3, 5, 2, 6, 1, 7)
 PLANE = tuple((a, b) for a in STEPS_X for b in STEPS + (0,) if a or b)
+FLAG_ROWS = 16
 AHEAD = 2
 CHUNK = 4
 STEP = CHUNK * FACE
@@ -76,9 +77,9 @@
 
 def section(
     scale,
-    down_ref, up_ref, table, vox_hbm, cot_hbm, w1_hbm, w2_hbm,
+    down_ref, up_ref, vox_hbm, cot_hbm, w1_hbm, w2_hbm,
     out, packed,
-    vox, cot, w1, w2, ax, ah, ag, wt, dslope, sums, st, ct,
+    vox, cot, w1, w2, ax, ah, ag, wt, dslope, slopes, sums, st, ct,
     up_send, down_send, from_lo, from_hi,
     part_sum, core_in, plane_out, plane_in, mid, cross,
     load_s, halo_s, halo_r, s0, r0, s1, r1, s2, r2, s3, r3, s4, r4,
@@ -156,6 +157,9 @@
     for at, (field, high, low) in enumerate(faces):
         up_send[at * FACE : (at + 1) * FACE] = face(field, up, high)
         down_send[at * FACE : (at + 1) * FACE] = face(field, down, low)
+    flags = (AHEAD + 1) * FACE
+    for buffer, slot in ((up_send, up), (down_send, down)):
+        buffer[flags:] = jnp.where(slot < 2, 1.0, 0.0) * jnp.ones((FLAG_ROWS, LANES), BF16)
     pl.semaphore_wait(barrier, len(partners))
     sent.append(send(up_send, from_lo, halo_s.at[0], halo_r.at[0], above))
     sent.append(send(down_send, from_hi, halo_s.at[1], halo_r.at[1], below))
@@ -171,11 +175,6 @@
 
         lax.fori_loop(0, 4, body, 0, unroll=True)
 
-    fill(vox, ax, AHEAD)
-
-    loads[2].wait()
-    loads[3].wait()
-
     def weights(n, carry):
         for k in range(3):
             o = 3 * n + k
@@ -184,29 +183,25 @@
             wt[26 - o] = square.T[:CH, :CH].astype(BF16)
         return carry
 
-    lax.fori_loop(0, 9, weights, 0, unroll=True)
-    fill(cot, ag, 1)
+    lower_valid = space > 0
+    upper_valid = space < owners - 1
 
     def cot_turn(c, carry):
         block = ag[pl.ds(pl.multiple_of(FACE + c * STEP, FACE), STEP), 3 * LANES : 4 * LANES]
         ct[:, pl.ds(pl.multiple_of(c * STEP, STEP), STEP)] = block.astype(F32).T[:CH].astype(BF16)
         return carry
 
-    lax.fori_loop(0, 4, cot_turn, 0, unroll=True)
-
-    def linked(slot, way):
-        entry = jnp.where(slot == 0, table[0, 0, way], jnp.where(slot == 1, table[0, 1, way], 3))
-        return entry == 2
-
-    lower_active, upper_active = linked(down, 1), linked(up, 7)
+    def neighbour(buffer, valid):
+        flag = buffer[flags : flags + FLAG_ROWS].astype(F32)[:1]
+        return jnp.where(valid, flag, 0.0) > 0.5
 
     def keep(value, planes):
         kept = []
         for k, plane in enumerate(planes):
             if plane < 0:
-                active = lower_active
+                active = neighbour(from_lo, lower_valid)
             elif plane >= PLANES:
-                active = upper_active
+                active = neighbour(from_hi, upper_valid)
             else:
                 active = (down if plane < EDGE else up) < 2
             kept.append(jnp.where(active, value[k * FACE : (k + 1) * FACE], 0.0))
@@ -252,42 +247,71 @@
         total = keep(convolve(ag, wt, planes, 1), planes)
         for k, first, count in runs(planes):
             rows = slice(first * FACE, (first + count) * FACE)
-            slope = total[k * FACE : (k + count) * FACE] * dslope[rows]
-            st[:, rows] = slope.T[:CH].astype(BF16)
-
-    inner = ((2, 3, 4, 5), (6, 7, 8, 9), (10, 11, 12, 13))
+            slopes[rows] = total[k * FACE : (k + count) * FACE] * dslope[rows]
+
+    def turn(pairs):
+        for pair in pairs:
+            rows = slice(pair * 2 * FACE, (pair + 1) * 2 * FACE)
+            st[:, rows] = slopes[rows].T[:CH].astype(BF16)
+
+    def gradient(turned, wide, g, ahead, k, inside):
+        i = k * core + (2 - k) * (1 - core)
+
+        def rows(plane, count):
+            return pl.ds(pl.multiple_of((i + ahead - 1 + plane) * FACE, FACE), count * FACE)
+
+        if inside:
+            left, right = turned[:, 2 * FACE : 14 * FACE], wide[rows(2, 12)]
+        else:
+            left = jnp.concatenate([turned[:, : 2 * FACE], turned[:, 14 * FACE :]], axis=1)
+            right = jnp.concatenate([wide[rows(0, 2)], wide[rows(14, 2)]], axis=0)
+        block = jnp.dot(left, right, preferred_element_type=F32)
+        for tile in range(TILES_WIDE):
+            at = pl.ds(pl.multiple_of((i * TILES_WIDE + tile) * CH, CH), CH)
+            part = block[:, LANES * tile : LANES * (tile + 1)]
+            part_sum[g, at] = part if inside else part_sum[g, at] + part
+
+    fill(vox, ax, AHEAD)
+    inner = ((1, 2, 3, 4), (5, 6, 7), (8, 9, 10), (11, 12, 13, 14))
+    loads[2].wait()
     for planes in inner:
         first_conv(planes)
+    loads[3].wait()
+    lax.fori_loop(0, 9, weights, 0, unroll=True)
+    fill(cot, ag, 1)
+    lax.fori_loop(0, 4, cot_turn, 0, unroll=True)
     for planes in inner:
         through(planes)
+    turn(range(1, 7))
+    used = 3 * TILES_WIDE * CH
+    for g in range(2):
+        part_sum[g, used:] = jnp.zeros((2 * HALF - used, LANES), F32)
+    for k in range(3):
+        gradient(st, ax, 0, AHEAD, k, True)
+    for k in range(3):
+        gradient(ct, ah, 1, 1, k, True)
 
     def edge_in(buffer, at, count, valid, wide, row):
         block = buffer[at * FACE : (at + count) * FACE].astype(F32)
         block = jnp.where(valid, block, 0.0).reshape(count, EDGE, EDGE, LANES)
         spread(block, wide, row)
 
-    lower_valid = space > 0
-    upper_valid = space < owners - 1
     arrived(from_lo, halo_s.at[0], halo_r.at[0], above)
+    arrived(from_hi, halo_s.at[1], halo_r.at[1], below)
     edge_in(from_lo, 0, AHEAD, lower_valid, ax, 0)
+    edge_in(from_hi, 0, AHEAD, upper_valid, ax, (PLANES + AHEAD) * FACE)
+    first_conv((-1, 0, 15, 16))
     edge_in(from_lo, AHEAD, 1, lower_valid, ag, 0)
-    arrived(from_hi, halo_s.at[1], halo_r.at[1], below)
-    edge_in(from_hi, 0, AHEAD, upper_valid, ax, (PLANES + AHEAD) * FACE)
     edge_in(from_hi, AHEAD, 1, upper_valid, ag, (PLANES + 1) * FACE)
-    first_conv((-1, 0, 1, 14, 15, 16))
-    through((0, 1, 14, 15))
+    through((0, 15))
+    turn((0, 7))
     centre = slice(3 * LANES, 4 * LANES)
-
-    def gradient(turned, wide, g, ahead, k):
-        i = k * core + (2 - k) * (1 - core)
-        rows = pl.ds(pl.multiple_of((i + ahead - 1) * FACE, FACE), ROWS)
-        block = jnp.dot(turned[...], wide[rows], preferred_element_type=F32)
-        for tile in range(TILES_WIDE):
-            at = pl.multiple_of((i * TILES_WIDE + tile) * CH, CH)
-            part_sum[g, pl.ds(at, CH)] = block[:, LANES * tile : LANES * (tile + 1)]
 
     def rows_of(start, count):
         return pl.ds(pl.multiple_of(start, SHARD), count)
+
+    def other(k, me):
+        return k + jnp.where(k >= me, 1, 0)
 
     def core_send(g):
         for a in STEPS_X:
@@ -320,34 +344,36 @@
             total = total + plane_in[g, n].astype(F32)
         cross[g, line] = total
         mine = cross.at[g, line]
-        for d in STEPS:
-            target = in_line(lax.rem(line + d, SIDE))
-            sent.append(send(mine, mine, s2.at[g, d], r2.at[g, d], target))
+        for k in range(SIDE - 1):
+            target = in_line(other(k, line))
+            sent.append(send(mine, mine, s2.at[g, k], r2.at[g, line], target))
 
     def place_of(x, t):
         return rows_of(core * HALF + x * GROUP + t * SHARD, SHARD)
 
     def line_add(g):
         for d in STEPS[::-1]:
-            theirs = cross.at[g, lax.rem(line + SIDE - d, SIDE)]
-            arrived(theirs, s2.at[g, d], r2.at[g, d], twin)
+            t = lax.rem(line + SIDE - d, SIDE)
+            arrived(cross.at[g, t], s2.at[g, d], r2.at[g, t], twin)
         total = cross[g, 0]
         for t in range(1, SIDE):
             total = total + cross[g, t]
         packed[g, place_of(my_x, side)] = (total * scale).astype(BF16)
         mine = packed.at[g, place_of(my_x, side)]
-        for a, b in PLANE:
-            n = a * SIDE + b
-            sent.append(send(mine, mine, s3.at[g, n], r3.at[g, n], in_plane(*moved(a, b))))
+        me = side * SIZE_X + my_x
+        for k in range(SIDE * SIZE_X - 1):
+            at = other(k, me)
+            target = in_plane(lax.rem(at, SIZE_X), lax.div(at, SIZE_X))
+            sent.append(send(mine, mine, s3.at[g, k], r3.at[g, me], target))
 
     def plane_gather(g):
         for a in STEPS_X[::-1]:
             x = lax.rem(my_x + SIZE_X - a, SIZE_X)
             for b in (0,) + STEPS[::-1]:
                 if (a, b) != (0, 0):
-                    n = a * SIDE + b
-                    theirs = packed.at[g, place_of(x, lax.rem(side + SIDE - b, SIDE))]
-                    arrived(theirs, s3.at[g, n], r3.at[g, n], twin)
+                    t = lax.rem(side + SIDE - b, SIDE)
+                    theirs = packed.at[g, place_of(x, t)]
+                    arrived(theirs, s3.at[g, 0], r3.at[g, t * SIZE_X + x], twin)
             group = packed.at[g, rows_of(core * HALF + x * GROUP, GROUP)]
             sent.append(send(group, group, s4.at[g, a], r4.at[g, a], twin))
 
@@ -357,18 +383,15 @@
             group = packed.at[g, rows_of((1 - core) * HALF + x * GROUP, GROUP)]
             arrived(group, s4.at[g, a], r4.at[g, a], twin)
 
-    used = 3 * TILES_WIDE * CH
-    for g in range(2):
-        part_sum[g, used:] = jnp.zeros((2 * HALF - used, LANES), F32)
-    gradient(st, ax, 0, AHEAD, 0)
-    gradient(st, ax, 0, AHEAD, 1)
+    gradient(st, ax, 0, AHEAD, 0, False)
+    gradient(st, ax, 0, AHEAD, 1, False)
     core_send(0)
-    gradient(st, ax, 0, AHEAD, 2)
-    gradient(ct, ah, 1, 1, 0)
-    gradient(ct, ah, 1, 1, 1)
+    gradient(st, ax, 0, AHEAD, 2, False)
+    gradient(ct, ah, 1, 1, 0, False)
+    gradient(ct, ah, 1, 1, 1, False)
     core_send(1)
     core_add(0)
-    gradient(ct, ah, 1, 1, 2)
+    gradient(ct, ah, 1, 1, 2, False)
     core_add(1)
 
     for planes in ((0, 1, 2, 3), (4, 5, 6, 7), (8, 9, 10, 11), (12, 13, 14, 15)):
@@ -419,14 +442,13 @@
     field, packed = pl.pallas_call(
         functools.partial(section, scale),
         out_shape=(field_shape, packed_shape),
-        in_specs=[smem, smem, smem] + [pl.BlockSpec(memory_space=pltpu.HBM)] * 4,
+        in_specs=[smem, smem] + [pl.BlockSpec(memory_space=pltpu.HBM)] * 4,
         out_specs=(vmem, vmem),
         scratch_shapes=[
             bricks, bricks, weight, weight, wider, wide, wide, weight,
-            pltpu.VMEM((ROWS, LANES), F32),
-            pltpu.VMEM((ROWS, LANES), F32),
+            *[pltpu.VMEM((ROWS, LANES), F32)] * 3,
             turned, turned,
-            *[pltpu.VMEM(((AHEAD + 1) * FACE, LANES), BF16)] * 4,
+            *[pltpu.VMEM(((AHEAD + 1) * FACE + FLAG_ROWS, LANES), BF16)] * 4,
             pltpu.VMEM((2, 2 * HALF, LANES), F32),
             pltpu.VMEM((2, HALF, LANES), F32),
             pltpu.VMEM((2, SIZE_X * SIDE, SHARD, LANES), BF16),
@@ -442,7 +464,7 @@
         ),
         name="section",
     )(
-        down_list, up_list, table,
+        down_list, up_list,
         *[
             pltpu.with_memory_space_constraint(array, pltpu.HBM)
             for array in (voxels[0], cotangent[0], weight_first, weight_second)

time: 57.9 us -> 54.2 us (0.936)
  Pallas kernels: 55.1 us -> 52.1 us
  local copies, waits for them, and re-layouts: 0.67 us -> 0 us
    pallas_call x1, Pallas kernels: 52.5 us -> 49.6 us  [on_device(): pl.pallas_call(functools.partial(section, scale), out_shape=(field_shape,...]
    unnamed x2 -> x0, local copies, waits for them, and re-layouts: 0.67 us -> none
where the time goes in v4:
time: 54.2 us; the launch traced here: 54 us
  Pallas kernels  52.1 us (96%)
  between operations  1.93 us (4%)
    pallas_call x1, Pallas kernels, on_device(): pl.pallas_call(functools.partial(section, scale), out_shape=(field_shape,...  49.6 us
    pallas_call x1, Pallas kernels, on_device(): pl.pallas_call(unpack, grid=(3,), out_shape=(jax.ShapeDtypeStruct((27 * C...  2.56 us

profile of v4, /device:TPU:1, one launch (start us, length us, event | category | flops | bytes accessed | tf_op | source)
XLA Modules:
  0.0 54.0 jit_solution(8001196739739370028)
XLA Ops:
  1.9 49.6 %section.1 = (bf16[2,8,8,8,96]{4,3,2,1,0:T(8,128)(2,1)S(1)}, bf16[2,2048,128]{2,1,0:T(8,128)(2,1)S(1)}) custom-call(s32[1,1]{1,0:T(1,128)S(6)} %copy.10.down_ref, s32[1,1]{1,0:T(1,128)S(6)} %copy.9.up_ref, bf16[2,8,8,8,96]{4,3,2,1,0:T(8,128)(2,1)} %bitcast.5, bf16[2,8,8,8,96]{4,3,2,1,0:T(8,128)(2,1)} %bitcast.6, bf16[27,96,96]{2,1,0:T(8,128)(2,1)} %w1_hbm.1, ...), custom_call_target="tpu_custom_call" | custom-call | tf_op jit(solution)/shard_map/section/pallas_call | solution.py:442
  51.5 2.6 %unpack.1 = (f32[2592,96]{1,0:T(8,128)}, f32[2592,96]{1,0:T(8,128)}, bf16[2,8,8,8,96]{4,3,2,1,0:T(8,128)(2,1)}) custom-call(bf16[2,2048,128]{2,1,0:T(8,128)(2,1)S(1)} %get-tuple-element.8.packed, bf16[2,8,8,8,96]{4,3,2,1,0:T(8,128)(2,1)S(1)} %get-tuple-element.9.field), custom_call_target="tpu_custom_call" | custom-call | tf_op jit(solution)/shard_map/unpack/pallas_call | solution.py:474

commit v5 on v4

--- a/solution.py
+++ b/solution.py
@@ -78,10 +78,10 @@
 def section(
     scale,
     down_ref, up_ref, vox_hbm, cot_hbm, w1_hbm, w2_hbm,
-    out, packed,
+    out, grad_first, grad_second,
     vox, cot, w1, w2, ax, ah, ag, wt, dslope, slopes, sums, st, ct,
     up_send, down_send, from_lo, from_hi,
-    part_sum, core_in, plane_out, plane_in, mid, cross,
+    part_sum, core_in, plane_out, plane_in, mid, cross, packed,
     load_s, halo_s, halo_r, s0, r0, s1, r1, s2, r2, s3, r3, s4, r4,
 ):
     space = lax.axis_index("space")
@@ -314,66 +314,52 @@
         return k + jnp.where(k >= me, 1, 0)
 
     def core_send(g):
-        for a in STEPS_X:
-            start = lax.rem(my_x + a, SIZE_X) * GROUP
-            src = part_sum.at[g, rows_of((1 - core) * HALF + start, GROUP)]
-            dst = core_in.at[g, rows_of(start, GROUP)]
-            sent.append(send(src, dst, s0.at[g, a], r0.at[g, a], twin))
+        src = part_sum.at[g, rows_of((1 - core) * HALF, HALF)]
+        sent.append(send(src, core_in.at[g], s0.at[g], r0.at[g], twin))
+
+    def all_sent(src, sem):
+        pltpu.make_async_copy(src, src, sem).wait()
 
     def core_add(g):
-        for a in STEPS_X:
-            start = lax.rem(my_x + a, SIZE_X) * GROUP
-            arrived(core_in.at[g, rows_of(start, GROUP)], s0.at[g, a], r0.at[g, a], twin)
-            for b in STEPS + (0,):
-                x, t = moved(a, b)
-                at = x * GROUP + t * SHARD
-                total = part_sum[g, rows_of(core * HALF + at, SHARD)] + core_in[g, rows_of(at, SHARD)]
-                if (a, b) == (0, 0):
-                    mid[g] = total
-                else:
-                    n = a * SIDE + b
-                    plane_out[g, n] = total.astype(BF16)
-                    src, dst = plane_out.at[g, n], plane_in.at[g, n]
-                    sent.append(send(src, dst, s1.at[g, n], r1.at[g, n], in_plane(x, t)))
+        arrived(core_in.at[g], s0.at[g], r0.at[g], twin)
+        for n, (a, b) in enumerate(PLANE):
+            x, t = moved(a, b)
+            at = x * GROUP + t * SHARD
+            total = part_sum[g, rows_of(core * HALF + at, SHARD)] + core_in[g, rows_of(at, SHARD)]
+            plane_out[g, n] = total.astype(BF16)
+            send(plane_out.at[g, n], plane_in.at[g, n], s1.at[g], r1.at[g], in_plane(x, t))
+        at = my_x * GROUP + side * SHARD
+        mid[g] = part_sum[g, rows_of(core * HALF + at, SHARD)] + core_in[g, rows_of(at, SHARD)]
 
     def plane_add(g):
+        arrived(plane_in.at[g], s1.at[g], r1.at[g], twin)
         total = mid[g]
-        for a, b in PLANE[::-1]:
-            n = a * SIDE + b
-            arrived(plane_in.at[g, n], s1.at[g, n], r1.at[g, n], twin)
+        for n in range(len(PLANE)):
             total = total + plane_in[g, n].astype(F32)
         cross[g, line] = total
         mine = cross.at[g, line]
         for k in range(SIDE - 1):
-            target = in_line(other(k, line))
-            sent.append(send(mine, mine, s2.at[g, k], r2.at[g, line], target))
-
-    def place_of(x, t):
-        return rows_of(core * HALF + x * GROUP + t * SHARD, SHARD)
+            send(mine, mine, s2.at[g], r2.at[g], in_line(other(k, line)))
 
     def line_add(g):
-        for d in STEPS[::-1]:
-            t = lax.rem(line + SIDE - d, SIDE)
-            arrived(cross.at[g, t], s2.at[g, d], r2.at[g, t], twin)
+        arrived(cross.at[g, : SIDE - 1], s2.at[g], r2.at[g], twin)
         total = cross[g, 0]
         for t in range(1, SIDE):
             total = total + cross[g, t]
-        packed[g, place_of(my_x, side)] = (total * scale).astype(BF16)
-        mine = packed.at[g, place_of(my_x, side)]
+        rows = rows_of(core * HALF + my_x * GROUP + side * SHARD, SHARD)
+        packed[g, rows] = (total * scale).astype(BF16)
+        mine = packed.at[g, rows]
         me = side * SIZE_X + my_x
         for k in range(SIDE * SIZE_X - 1):
             at = other(k, me)
             target = in_plane(lax.rem(at, SIZE_X), lax.div(at, SIZE_X))
-            sent.append(send(mine, mine, s3.at[g, k], r3.at[g, me], target))
+            send(mine, mine, s3.at[g], r3.at[g, my_x], target)
 
     def plane_gather(g):
         for a in STEPS_X[::-1]:
             x = lax.rem(my_x + SIZE_X - a, SIZE_X)
-            for b in (0,) + STEPS[::-1]:
-                if (a, b) != (0, 0):
-                    t = lax.rem(side + SIDE - b, SIDE)
-                    theirs = packed.at[g, place_of(x, t)]
-                    arrived(theirs, s3.at[g, 0], r3.at[g, t * SIZE_X + x], twin)
+            count = GROUP if a else GROUP - SHARD
+            arrived(packed.at[g, rows_of(core * HALF + x * GROUP, count)], s3.at[g], r3.at[g, x], twin)
             group = packed.at[g, rows_of(core * HALF + x * GROUP, GROUP)]
             sent.append(send(group, group, s4.at[g, a], r4.at[g, a], twin))
 
@@ -382,6 +368,13 @@
             x = lax.rem(my_x + SIZE_X - a, SIZE_X)
             group = packed.at[g, rows_of((1 - core) * HALF + x * GROUP, GROUP)]
             arrived(group, s4.at[g, a], r4.at[g, a], twin)
+        result = (grad_first, grad_second)[g]
+        for i in range(3):
+            for tile in range(TILES_WIDE):
+                at = (i * TILES_WIDE + tile) * CH
+                count = min(LANES, WIDE - LANES * tile)
+                start = i * WIDE + LANES * tile
+                result[start : start + count] = packed[g, at : at + CH].astype(F32).T[:count]
 
     gradient(st, ax, 0, AHEAD, 0, False)
     gradient(st, ax, 0, AHEAD, 1, False)
@@ -416,15 +409,22 @@
             stage(g)
     for copy in sent:
         copy.wait_send()
-
-
-def unpack(packed, field, first, second, out):
-    out[...] = field[...]
-    for g, result in enumerate((first, second)):
-        for tile in range(TILES_WIDE):
-            turned = packed[g, CH * tile : CH * (tile + 1)].astype(F32).T
-            count = min(LANES, WIDE - LANES * tile)
-            result[LANES * tile : LANES * tile + count] = turned[:count]
+    for g in range(2):
+        all_sent(plane_out.at[g], s1.at[g])
+        all_sent(cross.at[g, : SIDE - 1], s2.at[g])
+        all_sent(packed.at[g, : HALF - SHARD], s3.at[g])
+
+
+def store(*refs):
+    count = len(refs) // 2
+    copies = [
+        pltpu.make_async_copy(src, dst, refs[-1].at[n])
+        for n, (src, dst) in enumerate(zip(refs[:count], refs[count : 2 * count]))
+    ]
+    for copy in copies:
+        copy.start()
+    for copy in copies:
+        copy.wait()
 
 
 def on_device(voxels, cotangent, weight_first, weight_second, act_count, up_list, down_list, table):
@@ -433,17 +433,18 @@
     scale = 1.0 / math.sqrt(512 * 2 * EDGE**3)
     dma = pltpu.SemaphoreType.DMA
     field_shape = jax.ShapeDtypeStruct((2, EDGE, EDGE, EDGE, CH), BF16)
-    packed_shape = jax.ShapeDtypeStruct((2, 2 * HALF, LANES), BF16)
+    sum_shape = jax.ShapeDtypeStruct((27 * CH, CH), F32)
+    results = (field_shape, sum_shape, sum_shape)
     wide = pltpu.VMEM((ROWS + 2 * FACE, TILES_WIDE * LANES), BF16)
     wider = pltpu.VMEM((ROWS + 2 * AHEAD * FACE, TILES_WIDE * LANES), BF16)
     weight = pltpu.VMEM((27, CH, CH), BF16)
     bricks = pltpu.VMEM(field_shape.shape, BF16)
     turned = pltpu.VMEM((CH, ROWS), BF16)
-    field, packed = pl.pallas_call(
+    held = pl.pallas_call(
         functools.partial(section, scale),
-        out_shape=(field_shape, packed_shape),
+        out_shape=results,
         in_specs=[smem, smem] + [pl.BlockSpec(memory_space=pltpu.HBM)] * 4,
-        out_specs=(vmem, vmem),
+        out_specs=(vmem,) * 3,
         scratch_shapes=[
             bricks, bricks, weight, weight, wider, wide, wide, weight,
             *[pltpu.VMEM((ROWS, LANES), F32)] * 3,
@@ -451,13 +452,12 @@
             *[pltpu.VMEM(((AHEAD + 1) * FACE + FLAG_ROWS, LANES), BF16)] * 4,
             pltpu.VMEM((2, 2 * HALF, LANES), F32),
             pltpu.VMEM((2, HALF, LANES), F32),
-            pltpu.VMEM((2, SIZE_X * SIDE, SHARD, LANES), BF16),
-            pltpu.VMEM((2, SIZE_X * SIDE, SHARD, LANES), BF16),
+            *[pltpu.VMEM((2, len(PLANE), SHARD, LANES), BF16)] * 2,
             pltpu.VMEM((2, SHARD, LANES), F32),
             pltpu.VMEM((2, SIDE, SHARD, LANES), F32),
+            pltpu.VMEM((2, 2 * HALF, LANES), BF16),
             dma((4,)), dma((2,)), dma((2,)),
-            *[dma((2, SIZE_X))] * 2, *[dma((2, SIZE_X * SIDE))] * 2,
-            *[dma((2, SIDE))] * 2, *[dma((2, SIZE_X * SIDE))] * 2, *[dma((2, SIZE_X))] * 2,
+            *[dma((2,))] * 7, dma((2, SIZE_X)), *[dma((2, SIZE_X))] * 2,
         ],
         compiler_params=pltpu.CompilerParams(
             collective_id=0, has_side_effects=True, vmem_limit_bytes=48 * 2**20
@@ -470,23 +470,15 @@
             for array in (voxels[0], cotangent[0], weight_first, weight_second)
         ],
     )
-    step_rows = TILES_WIDE * CH
-    first, second, out_field = pl.pallas_call(
-        unpack,
-        grid=(3,),
-        out_shape=(jax.ShapeDtypeStruct((27 * CH, CH), F32),) * 2 + (field_shape,),
-        in_specs=[
-            pl.BlockSpec((2, step_rows, LANES), lambda i: (0, i, 0)),
-            pl.BlockSpec(field_shape.shape, lambda i: (0, 0, 0, 0, 0)),
-        ],
-        out_specs=(
-            pl.BlockSpec((WIDE, CH), lambda i: (i, 0)),
-            pl.BlockSpec((WIDE, CH), lambda i: (i, 0)),
-            pl.BlockSpec(field_shape.shape, lambda i: (0, 0, 0, 0, 0)),
-        ),
-        compiler_params=pltpu.CompilerParams(vmem_limit_bytes=32 * 2**20),
-        name="unpack",
-    )(packed, field)
+    out_field, first, second = pl.pallas_call(
+        store,
+        out_shape=results,
+        in_specs=[vmem] * 3,
+        out_specs=(pl.BlockSpec(memory_space=pltpu.HBM),) * 3,
+        scratch_shapes=[dma((3,))],
+        compiler_params=pltpu.CompilerParams(vmem_limit_bytes=8 * 2**20),
+        name="store",
+    )(*held)
     shape = weight_first.shape
     return (out_field[None], first.reshape(shape), second.reshape(shape))
 

time: 54.2 us -> 50.8 us (0.937)
  Pallas kernels: 52.1 us -> 48.7 us
    pallas_call x2, Pallas kernels: 52.1 us -> 48.7 us  [the longest x1 47.1 us: on_device(): pl.pallas_call(functools.partial(section, scale), out_shape=results, in_s...]
where the time goes in v5:
time: 50.8 us; the launch traced here: 50.6 us
  Pallas kernels  48.7 us (96%)
  between operations  1.93 us (4%)
    pallas_call x1, Pallas kernels, on_device(): pl.pallas_call(functools.partial(section, scale), out_shape=results, in_s...  47.1 us
    pallas_call x1, Pallas kernels, on_device(): pl.pallas_call(store, out_shape=results, in_specs=[vmem] * 3, out_specs=(...  1.61 us

profile of v5, /device:TPU:1, one launch (start us, length us, event | category | flops | bytes accessed | tf_op | source)
XLA Modules:
  0.0 50.6 jit_solution(15200828817351149760)
XLA Ops:
  1.9 47.1 %section.1 = (bf16[2,8,8,8,96]{4,3,2,1,0:T(8,128)(2,1)S(1)}, f32[2592,96]{1,0:T(8,128)S(1)}, f32[2592,96]{1,0:T(8,128)S(1)}) custom-call(s32[1,1]{1,0:T(1,128)S(6)} %copy.10.down_ref, s32[1,1]{1,0:T(1,128)S(6)} %copy.9.up_ref, bf16[2,8,8,8,96]{4,3,2,1,0:T(8,128)(2,1)} %bitcast.5, bf16[2,8,8,8,96]{4,3,2,1,0:T(8,128)(2,1)} %bitcast.6, ...), custom_call_target="tpu_custom_call" | custom-call | tf_op jit(solution)/shard_map/section/pallas_call | solution.py:443
  49.0 1.6 %store.1 = (bf16[2,8,8,8,96]{4,3,2,1,0:T(8,128)(2,1)}, f32[2592,96]{1,0:T(8,128)}, f32[2592,96]{1,0:T(8,128)}) custom-call(bf16[2,8,8,8,96]{4,3,2,1,0:T(8,128)(2,1)S(1)} %get-tuple-element.9.refs_0_, f32[2592,96]{1,0:T(8,128)S(1)} %get-tuple-element.10.refs_1_, f32[2592,96]{1,0:T(8,128)S(1)} %get-tuple-element.11.refs_2_), custom_call_target="tpu_custom_call" | custom-call | tf_op jit(solution)/shard_map/store/pallas_call | solution.py:473

commit v6 on v5

--- a/solution.py
+++ b/solution.py
@@ -20,6 +20,7 @@
 PLANES = 2 * EDGE
 ROWS = PLANES * FACE
 WIDE = 9 * CH
+TALL = 3 * CH
 TILES_WIDE = 7
 HALF = 1024
 GROUP = HALF // SIZE_X
@@ -40,23 +41,27 @@
     return jnp.concatenate([value, blank], axis=-1)
 
 
+def shifted(value, step):
+    if step == 0:
+        return value
+    deep = value.reshape(-1, EDGE, LANES)
+    depth = lax.broadcasted_iota(jnp.int32, deep.shape, 1)
+    if step > 0:
+        moved = jnp.where(depth == EDGE - 1, 0.0, pltpu.roll(deep, EDGE - 1, 1))
+    else:
+        moved = jnp.where(depth == 0, 0.0, pltpu.roll(deep, 1, 1))
+    return moved.reshape(value.shape)
+
+
 def spread(value, out, row):
-    planes = value.shape[0]
-    flat = value.reshape(planes * EDGE, EDGE, LANES)
-    depth = lax.broadcasted_iota(jnp.int32, flat.shape, 1)
-    by_depth = [
-        jnp.where(depth == 0, 0.0, pltpu.roll(flat, 1, 1)),
-        flat,
-        jnp.where(depth == EDGE - 1, 0.0, pltpu.roll(flat, EDGE - 1, 1)),
-    ]
+    planes = value.shape[0] - 2
+    flat = value.reshape(-1, LANES)
+    turns = {turn: pltpu.roll(flat, turn, 1).reshape(value.shape) for turn in (32, 64, 96)}
+    turns[0] = value
 
     def piece(index):
-        shift_y, shift_z = index // 3, index % 3
-        turned = by_depth[shift_z]
-        turn = CH * index % LANES
-        if turn:
-            turned = pltpu.roll(turned, turn, 2)
-        turned = turned.reshape(planes, EDGE, EDGE, LANES)
+        shift_x, shift_y = index // 3, index % 3
+        turned = turns[CH * index % LANES][shift_x : shift_x + planes]
         blank = jnp.zeros((planes, 1, EDGE, LANES), F32)
         if shift_y == 0:
             turned = jnp.concatenate([blank, turned[:, : EDGE - 1]], axis=1)
@@ -72,14 +77,14 @@
         block = pieces[first]
         if border < LANES and first + 1 < 9:
             block = jnp.where(lane < border, block, pieces[first + 1])
-        out[pl.ds(row, planes * FACE), LANES * tile : LANES * (tile + 1)] = block.astype(BF16)
+        out[row : row + planes * FACE, LANES * tile : LANES * (tile + 1)] = block.astype(BF16)
 
 
 def section(
     scale,
     down_ref, up_ref, vox_hbm, cot_hbm, w1_hbm, w2_hbm,
     out, grad_first, grad_second,
-    vox, cot, w1, w2, ax, ah, ag, wt, dslope, slopes, sums, st, ct,
+    vox, cot, w1, w2, fx, fh, fg, bx, bh, bg, c1, c2, ct2, dslope, slopes, sums, st, ct,
     up_send, down_send, from_lo, from_hi,
     part_sum, core_in, plane_out, plane_in, mid, cross, packed,
     load_s, halo_s, halo_r, s0, r0, s1, r1, s2, r2, s3, r3, s4, r4,
@@ -132,7 +137,7 @@
             ((vox_hbm, vox), (cot_hbm, cot), (w1_hbm, w1), (w2_hbm, w2))
         )
     ]
-    for load in loads:
+    for load in loads[:2]:
         load.start()
 
     barrier = pltpu.get_barrier_semaphore()
@@ -142,54 +147,44 @@
     for partner in partners:
         pl.semaphore_signal(barrier, inc=1, device_id=partner, device_id_type=MESH)
 
+    for load in loads[2:]:
+        load.start()
     down = down_ref[0, 0]
     up = up_ref[0, 0]
     sent = []
-
-    def face(field, slot, plane):
-        first, second = widen(field[0, plane]), widen(field[1, plane])
-        chosen = jnp.where(slot == 0, first, jnp.where(slot == 1, second, 0.0))
-        return chosen.reshape(FACE, LANES).astype(BF16)
+    for joined in (c1, c2, ct2):
+        joined[...] = jnp.zeros(joined.shape, BF16)
+
+    def fill(field, planes, ahead):
+        for slot, start in ((down, 0), (up, EDGE)):
+            for at in range(0, EDGE, CHUNK):
+                one, two = (widen(field[n, at : at + CHUNK]) for n in range(2))
+                chosen = jnp.where(slot == 0, one, jnp.where(slot == 1, two, 0.0))
+                row = (ahead + start + at) * FACE
+                planes[row : row + STEP] = chosen.reshape(STEP, LANES)
 
     loads[0].wait()
+    fill(vox, fx, AHEAD)
     loads[1].wait()
-    faces = ((vox, EDGE - 2, 0), (vox, EDGE - 1, 1), (cot, EDGE - 1, 0))
-    for at, (field, high, low) in enumerate(faces):
-        up_send[at * FACE : (at + 1) * FACE] = face(field, up, high)
-        down_send[at * FACE : (at + 1) * FACE] = face(field, down, low)
+    fill(cot, fg, 1)
     flags = (AHEAD + 1) * FACE
-    for buffer, slot in ((up_send, up), (down_send, down)):
+    for buffer, slot, high, low in (
+        (up_send, up, PLANES - AHEAD, PLANES - 1), (down_send, down, 0, 0)
+    ):
+        row = (AHEAD + high) * FACE
+        buffer[: AHEAD * FACE] = fx[row : row + AHEAD * FACE].astype(BF16)
+        buffer[AHEAD * FACE : flags] = fg[(1 + low) * FACE : (2 + low) * FACE].astype(BF16)
         buffer[flags:] = jnp.where(slot < 2, 1.0, 0.0) * jnp.ones((FLAG_ROWS, LANES), BF16)
     pl.semaphore_wait(barrier, len(partners))
     sent.append(send(up_send, from_lo, halo_s.at[0], halo_r.at[0], above))
     sent.append(send(down_send, from_hi, halo_s.at[1], halo_r.at[1], below))
 
-    def fill(field, wide, ahead):
-        def body(c, carry):
-            planes = pl.ds(lax.rem(c, 2) * CHUNK, CHUNK)
-            slot = jnp.where(c < 2, down, up)
-            first, second = widen(field[0, planes]), widen(field[1, planes])
-            chosen = jnp.where(slot == 0, first, jnp.where(slot == 1, second, 0.0))
-            spread(chosen, wide, pl.multiple_of(ahead * FACE + c * STEP, FACE))
-            return carry
-
-        lax.fori_loop(0, 4, body, 0, unroll=True)
-
-    def weights(n, carry):
-        for k in range(3):
-            o = 3 * n + k
-            own = widen(w2[o])
-            square = jnp.concatenate([own, jnp.zeros((LANES - CH, LANES), F32)], axis=0)
-            wt[26 - o] = square.T[:CH, :CH].astype(BF16)
-        return carry
+    def join(offset, value, joined):
+        pair, depth = offset // 3, offset % 3
+        joined[pair * CH : (pair + 1) * CH, LANES * depth : LANES * depth + CH] = value
 
     lower_valid = space > 0
     upper_valid = space < owners - 1
-
-    def cot_turn(c, carry):
-        block = ag[pl.ds(pl.multiple_of(FACE + c * STEP, FACE), STEP), 3 * LANES : 4 * LANES]
-        ct[:, pl.ds(pl.multiple_of(c * STEP, STEP), STEP)] = block.astype(F32).T[:CH].astype(BF16)
-        return carry
 
     def neighbour(buffer, valid):
         flag = buffer[flags : flags + FLAG_ROWS].astype(F32)[:1]
@@ -216,49 +211,52 @@
                 found.append([k, plane, 1])
         return found
 
-    def convolve(wide, weight, planes, ahead):
-        total = None
-        for i in range(3):
-            rows = [
-                wide[(first + ahead - 1 + i) * FACE : (first + ahead - 1 + i + count) * FACE, :WIDE]
-                for _, first, count in runs(planes)
-            ]
-            product = jnp.dot(
-                rows[0] if len(rows) == 1 else jnp.concatenate(rows, axis=0),
-                weight[9 * i : 9 * i + 9].reshape(WIDE, CH),
-                preferred_element_type=F32,
-            )
-            total = product if total is None else total + product
-        return widen(total)
+    def widened(source, ahead, wide, wide_ahead, planes):
+        for _, first, count in runs(planes):
+            rows = slice((first - 1 + ahead) * FACE, (first + 1 + count + ahead) * FACE)
+            value = source[rows].reshape(count + 2, EDGE, EDGE, LANES)
+            spread(value, wide, (first + wide_ahead) * FACE)
+
+    def convolve(wide, joined, planes, ahead):
+        rows = [
+            wide[(first + ahead) * FACE : (first + ahead + count) * FACE, :WIDE]
+            for _, first, count in runs(planes)
+        ]
+        rows = rows[0] if len(rows) == 1 else jnp.concatenate(rows, axis=0)
+        product = jnp.dot(rows, joined[...], preferred_element_type=F32)
+        parts = [product[:, LANES * k : LANES * (k + 1)] for k in range(3)]
+        return shifted(parts[0], -1) + parts[1] + shifted(parts[2], 1)
 
     def first_conv(planes):
-        before = keep(convolve(ax, w1, planes, AHEAD), planes)
+        widened(fx, AHEAD, bx, 1, planes)
+        before = keep(convolve(bx, c1, planes, 1), planes)
         gate = jax.nn.sigmoid(before)
         factor = gate * (1.0 + before * (1.0 - gate))
         hidden = (before * gate).astype(BF16).astype(F32)
         for k, plane in enumerate(planes):
+            part = slice(k * FACE, (k + 1) * FACE)
             if 0 <= plane < PLANES:
-                dslope[plane * FACE : (plane + 1) * FACE] = factor[k * FACE : (k + 1) * FACE]
-        for k, first, count in runs(planes):
-            block = hidden[k * FACE : (k + count) * FACE].reshape(count, EDGE, EDGE, LANES)
-            spread(block, ah, (first + 1) * FACE)
+                dslope[plane * FACE : (plane + 1) * FACE] = factor[part]
+            fh[(plane + 1) * FACE : (plane + 2) * FACE] = hidden[part]
 
     def through(planes):
-        total = keep(convolve(ag, wt, planes, 1), planes)
+        widened(fg, 1, bg, 0, planes)
+        total = keep(convolve(bg, ct2, planes, 0), planes)
         for k, first, count in runs(planes):
             rows = slice(first * FACE, (first + count) * FACE)
             slopes[rows] = total[k * FACE : (k + count) * FACE] * dslope[rows]
 
-    def turn(pairs):
+    def turn(source, ahead, turned, pairs):
         for pair in pairs:
             rows = slice(pair * 2 * FACE, (pair + 1) * 2 * FACE)
-            st[:, rows] = slopes[rows].T[:CH].astype(BF16)
-
-    def gradient(turned, wide, g, ahead, k, inside):
-        i = k * core + (2 - k) * (1 - core)
-
+            value = source[(2 * pair + ahead) * FACE : (2 * pair + 2 + ahead) * FACE]
+            for depth in range(3):
+                block = shifted(value, 1 - depth).T[:CH]
+                turned[depth * CH : (depth + 1) * CH, rows] = block.astype(BF16)
+
+    def gradient(turned, wide, g, ahead, inside):
         def rows(plane, count):
-            return pl.ds(pl.multiple_of((i + ahead - 1 + plane) * FACE, FACE), count * FACE)
+            return slice((ahead + plane) * FACE, (ahead + plane + count) * FACE)
 
         if inside:
             left, right = turned[:, 2 * FACE : 14 * FACE], wide[rows(2, 12)]
@@ -267,45 +265,49 @@
             right = jnp.concatenate([wide[rows(0, 2)], wide[rows(14, 2)]], axis=0)
         block = jnp.dot(left, right, preferred_element_type=F32)
         for tile in range(TILES_WIDE):
-            at = pl.ds(pl.multiple_of((i * TILES_WIDE + tile) * CH, CH), CH)
+            at = slice(tile * TALL, (tile + 1) * TALL)
             part = block[:, LANES * tile : LANES * (tile + 1)]
             part_sum[g, at] = part if inside else part_sum[g, at] + part
 
-    fill(vox, ax, AHEAD)
     inner = ((1, 2, 3, 4), (5, 6, 7), (8, 9, 10), (11, 12, 13, 14))
     loads[2].wait()
+    for offset in range(27):
+        join(offset, w1[offset], c1)
     for planes in inner:
         first_conv(planes)
     loads[3].wait()
-    lax.fori_loop(0, 9, weights, 0, unroll=True)
-    fill(cot, ag, 1)
-    lax.fori_loop(0, 4, cot_turn, 0, unroll=True)
+    for offset in range(27):
+        own = widen(w2[offset])
+        square = jnp.concatenate([own, jnp.zeros((LANES - CH, LANES), F32)], axis=0)
+        join(26 - offset, square.T[:CH, :CH].astype(BF16), ct2)
     for planes in inner:
         through(planes)
-    turn(range(1, 7))
-    used = 3 * TILES_WIDE * CH
+    turn(fg, 1, ct, range(8))
+    turn(slopes, 0, st, range(1, 7))
+    for planes in ((2, 3, 4), (5, 6, 7), (8, 9, 10), (11, 12, 13)):
+        widened(fh, 1, bh, 0, planes)
+    used = TILES_WIDE * TALL
     for g in range(2):
         part_sum[g, used:] = jnp.zeros((2 * HALF - used, LANES), F32)
-    for k in range(3):
-        gradient(st, ax, 0, AHEAD, k, True)
-    for k in range(3):
-        gradient(ct, ah, 1, 1, k, True)
-
-    def edge_in(buffer, at, count, valid, wide, row):
+    gradient(st, bx, 0, 1, True)
+    gradient(ct, bh, 1, 0, True)
+    for offset in range(27):
+        join(offset, w2[offset], c2)
+
+    def edge_in(buffer, at, count, valid, planes, row):
         block = buffer[at * FACE : (at + count) * FACE].astype(F32)
-        block = jnp.where(valid, block, 0.0).reshape(count, EDGE, EDGE, LANES)
-        spread(block, wide, row)
+        planes[row : row + count * FACE] = jnp.where(valid, block, 0.0)
 
     arrived(from_lo, halo_s.at[0], halo_r.at[0], above)
     arrived(from_hi, halo_s.at[1], halo_r.at[1], below)
-    edge_in(from_lo, 0, AHEAD, lower_valid, ax, 0)
-    edge_in(from_hi, 0, AHEAD, upper_valid, ax, (PLANES + AHEAD) * FACE)
+    edge_in(from_lo, 0, AHEAD, lower_valid, fx, 0)
+    edge_in(from_hi, 0, AHEAD, upper_valid, fx, (PLANES + AHEAD) * FACE)
+    edge_in(from_lo, AHEAD, 1, lower_valid, fg, 0)
+    edge_in(from_hi, AHEAD, 1, upper_valid, fg, (PLANES + 1) * FACE)
     first_conv((-1, 0, 15, 16))
-    edge_in(from_lo, AHEAD, 1, lower_valid, ag, 0)
-    edge_in(from_hi, AHEAD, 1, upper_valid, ag, (PLANES + 1) * FACE)
     through((0, 15))
-    turn((0, 7))
-    centre = slice(3 * LANES, 4 * LANES)
+    turn(slopes, 0, st, (0, 7))
+    widened(fh, 1, bh, 0, (0, 1, 14, 15))
 
     def rows_of(start, count):
         return pl.ds(pl.multiple_of(start, SHARD), count)
@@ -314,16 +316,21 @@
         return k + jnp.where(k >= me, 1, 0)
 
     def core_send(g):
-        src = part_sum.at[g, rows_of((1 - core) * HALF, HALF)]
-        sent.append(send(src, core_in.at[g], s0.at[g], r0.at[g], twin))
+        for a in STEPS_X:
+            start = lax.rem(my_x + a, SIZE_X) * GROUP
+            src = part_sum.at[g, rows_of((1 - core) * HALF + start, GROUP)]
+            dst = core_in.at[g, rows_of(start, GROUP)]
+            sent.append(send(src, dst, s0.at[g, a], r0.at[g, a], twin))
 
     def all_sent(src, sem):
         pltpu.make_async_copy(src, src, sem).wait()
 
     def core_add(g):
-        arrived(core_in.at[g], s0.at[g], r0.at[g], twin)
         for n, (a, b) in enumerate(PLANE):
             x, t = moved(a, b)
+            if b == STEPS[0]:
+                group = core_in.at[g, rows_of(x * GROUP, GROUP)]
+                arrived(group, s0.at[g, a], r0.at[g, a], twin)
             at = x * GROUP + t * SHARD
             total = part_sum[g, rows_of(core * HALF + at, SHARD)] + core_in[g, rows_of(at, SHARD)]
             plane_out[g, n] = total.astype(BF16)
@@ -369,29 +376,29 @@
             group = packed.at[g, rows_of((1 - core) * HALF + x * GROUP, GROUP)]
             arrived(group, s4.at[g, a], r4.at[g, a], twin)
         result = (grad_first, grad_second)[g]
-        for i in range(3):
-            for tile in range(TILES_WIDE):
-                at = (i * TILES_WIDE + tile) * CH
-                count = min(LANES, WIDE - LANES * tile)
-                start = i * WIDE + LANES * tile
-                result[start : start + count] = packed[g, at : at + CH].astype(F32).T[:count]
-
-    gradient(st, ax, 0, AHEAD, 0, False)
-    gradient(st, ax, 0, AHEAD, 1, False)
+        for tile in range(TILES_WIDE):
+            for depth in range(3):
+                at = tile * TALL + depth * CH
+                block = packed[g, at : at + CH].astype(F32).T
+                low = LANES * tile
+                for pair in range(9):
+                    begin, end = max(low, CH * pair), min(low + LANES, CH * (pair + 1))
+                    if begin < end:
+                        row = (3 * pair + depth) * CH + begin - CH * pair
+                        result[row : row + end - begin] = block[begin - low : end - low]
+
+    gradient(st, bx, 0, 1, False)
     core_send(0)
-    gradient(st, ax, 0, AHEAD, 2, False)
-    gradient(ct, ah, 1, 1, 0, False)
-    gradient(ct, ah, 1, 1, 1, False)
+    gradient(ct, bh, 1, 0, False)
     core_send(1)
     core_add(0)
-    gradient(ct, ah, 1, 1, 2, False)
     core_add(1)
 
     for planes in ((0, 1, 2, 3), (4, 5, 6, 7), (8, 9, 10, 11), (12, 13, 14, 15)):
-        first, count = planes[0], len(planes)
-        total = convolve(ah, w2, planes, 1)
-        inputs = ax[(first + AHEAD) * FACE : (first + AHEAD + count) * FACE, centre].astype(F32)
-        sums[first * FACE : (first + count) * FACE] = keep(total + inputs, planes)
+        start, count = planes[0], len(planes)
+        total = convolve(bh, c2, planes, 0)
+        inputs = fx[(start + AHEAD) * FACE : (start + AHEAD + count) * FACE]
+        sums[start * FACE : (start + count) * FACE] = keep(total + inputs, planes)
 
     def place(n, carry):
         low = sums[pl.ds(pl.multiple_of(n * STEP, STEP), STEP)]
@@ -435,18 +442,19 @@
     field_shape = jax.ShapeDtypeStruct((2, EDGE, EDGE, EDGE, CH), BF16)
     sum_shape = jax.ShapeDtypeStruct((27 * CH, CH), F32)
     results = (field_shape, sum_shape, sum_shape)
-    wide = pltpu.VMEM((ROWS + 2 * FACE, TILES_WIDE * LANES), BF16)
-    wider = pltpu.VMEM((ROWS + 2 * AHEAD * FACE, TILES_WIDE * LANES), BF16)
+    planes = [pltpu.VMEM((ROWS + 2 * n * FACE, LANES), F32) for n in (AHEAD, 1, 1)]
+    wide = [pltpu.VMEM((ROWS + 2 * n * FACE, TILES_WIDE * LANES), BF16) for n in (1, 0, 0)]
+    joined = pltpu.VMEM((WIDE, 3 * LANES), BF16)
     weight = pltpu.VMEM((27, CH, CH), BF16)
     bricks = pltpu.VMEM(field_shape.shape, BF16)
-    turned = pltpu.VMEM((CH, ROWS), BF16)
+    turned = pltpu.VMEM((TALL, ROWS), BF16)
     held = pl.pallas_call(
         functools.partial(section, scale),
         out_shape=results,
         in_specs=[smem, smem] + [pl.BlockSpec(memory_space=pltpu.HBM)] * 4,
         out_specs=(vmem,) * 3,
         scratch_shapes=[
-            bricks, bricks, weight, weight, wider, wide, wide, weight,
+            bricks, bricks, weight, weight, *planes, *wide, joined, joined, joined,
             *[pltpu.VMEM((ROWS, LANES), F32)] * 3,
             turned, turned,
             *[pltpu.VMEM(((AHEAD + 1) * FACE + FLAG_ROWS, LANES), BF16)] * 4,
@@ -457,7 +465,7 @@
             pltpu.VMEM((2, SIDE, SHARD, LANES), F32),
             pltpu.VMEM((2, 2 * HALF, LANES), BF16),
             dma((4,)), dma((2,)), dma((2,)),
-            *[dma((2,))] * 7, dma((2, SIZE_X)), *[dma((2, SIZE_X))] * 2,
+            *[dma((2, SIZE_X))] * 2, *[dma((2,))] * 5, *[dma((2, SIZE_X))] * 3,
         ],
         compiler_params=pltpu.CompilerParams(
             collective_id=0, has_side_effects=True, vmem_limit_bytes=48 * 2**20

time: 50.8 us -> 49.4 us (0.972)
  Pallas kernels: 48.7 us -> 47.2 us
    pallas_call x1, Pallas kernels: 47.1 us -> 45.5 us  [on_device(): pl.pallas_call(functools.partial(section, scale), out_shape=results, in_s...]
where the time goes in v6:
time: 49.4 us; the launch traced here: 49.1 us
  Pallas kernels  47.2 us (96%)
  between operations  1.93 us (4%)
    pallas_call x1, Pallas kernels, on_device(): pl.pallas_call(functools.partial(section, scale), out_shape=results, in_s...  45.5 us
    pallas_call x1, Pallas kernels, on_device(): pl.pallas_call(store, out_shape=results, in_specs=[vmem] * 3, out_specs=(...  1.61 us

profile of v6, /device:TPU:1, one launch (start us, length us, event | category | flops | bytes accessed | tf_op | source)
XLA Modules:
  0.0 49.1 jit_solution(356462563451747106)
XLA Ops:
  1.9 45.5 %section.1 = (bf16[2,8,8,8,96]{4,3,2,1,0:T(8,128)(2,1)S(1)}, f32[2592,96]{1,0:T(8,128)S(1)}, f32[2592,96]{1,0:T(8,128)S(1)}) custom-call(s32[1,1]{1,0:T(1,128)S(6)} %copy.10.down_ref, s32[1,1]{1,0:T(1,128)S(6)} %copy.9.up_ref, bf16[2,8,8,8,96]{4,3,2,1,0:T(8,128)(2,1)} %bitcast.5, bf16[2,8,8,8,96]{4,3,2,1,0:T(8,128)(2,1)} %bitcast.6, ...), custom_call_target="tpu_custom_call" | custom-call | tf_op jit(solution)/shard_map/section/pallas_call | solution.py:451
  47.5 1.6 %store.1 = (bf16[2,8,8,8,96]{4,3,2,1,0:T(8,128)(2,1)}, f32[2592,96]{1,0:T(8,128)}, f32[2592,96]{1,0:T(8,128)}) custom-call(bf16[2,8,8,8,96]{4,3,2,1,0:T(8,128)(2,1)S(1)} %get-tuple-element.9.refs_0_, f32[2592,96]{1,0:T(8,128)S(1)} %get-tuple-element.10.refs_1_, f32[2592,96]{1,0:T(8,128)S(1)} %get-tuple-element.11.refs_2_), custom_call_target="tpu_custom_call" | custom-call | tf_op jit(solution)/shard_map/store/pallas_call | solution.py:481

commit v7 on v6

--- a/solution.py
+++ b/solution.py
@@ -31,6 +31,8 @@
 PLANE = tuple((a, b) for a in STEPS_X for b in STEPS + (0,) if a or b)
 FLAG_ROWS = 16
 AHEAD = 2
+BLOCKS = (tuple(range(21)), tuple(range(11, 21)) + tuple(range(11)))
+WHOLE = 10
 CHUNK = 4
 STEP = CHUNK * FACE
 
@@ -305,8 +307,6 @@
     edge_in(from_lo, AHEAD, 1, lower_valid, fg, 0)
     edge_in(from_hi, AHEAD, 1, upper_valid, fg, (PLANES + 1) * FACE)
     first_conv((-1, 0, 15, 16))
-    through((0, 15))
-    turn(slopes, 0, st, (0, 7))
     widened(fh, 1, bh, 0, (0, 1, 14, 15))
 
     def rows_of(start, count):
@@ -346,7 +346,8 @@
         cross[g, line] = total
         mine = cross.at[g, line]
         for k in range(SIDE - 1):
-            send(mine, mine, s2.at[g], r2.at[g], in_line(other(k, line)))
+            t = other(k, line) * core + lax.rem(line + STEPS[k], SIDE) * (1 - core)
+            send(mine, mine, s2.at[g], r2.at[g], in_line(t))
 
     def line_add(g):
         arrived(cross.at[g, : SIDE - 1], s2.at[g], r2.at[g], twin)
@@ -359,7 +360,10 @@
         me = side * SIZE_X + my_x
         for k in range(SIDE * SIZE_X - 1):
             at = other(k, me)
-            target = in_plane(lax.rem(at, SIZE_X), lax.div(at, SIZE_X))
+            x, t = moved(*PLANE[k])
+            x = lax.rem(at, SIZE_X) * (1 - core) + x * core
+            t = lax.div(at, SIZE_X) * (1 - core) + t * core
+            target = in_plane(x, t)
             send(mine, mine, s3.at[g], r3.at[g, my_x], target)
 
     def plane_gather(g):
@@ -369,30 +373,36 @@
             arrived(packed.at[g, rows_of(core * HALF + x * GROUP, count)], s3.at[g], r3.at[g, x], twin)
             group = packed.at[g, rows_of(core * HALF + x * GROUP, GROUP)]
             sent.append(send(group, group, s4.at[g, a], r4.at[g, a], twin))
+        for c in range(2):
+            pl.when(core == c)(functools.partial(results, g, BLOCKS[c][:WHOLE]))
 
     def core_gather(g):
         for a in STEPS_X[::-1]:
             x = lax.rem(my_x + SIZE_X - a, SIZE_X)
             group = packed.at[g, rows_of((1 - core) * HALF + x * GROUP, GROUP)]
             arrived(group, s4.at[g, a], r4.at[g, a], twin)
+        for c in range(2):
+            pl.when(core == c)(functools.partial(results, g, BLOCKS[c][WHOLE:]))
+
+    def results(g, blocks):
         result = (grad_first, grad_second)[g]
-        for tile in range(TILES_WIDE):
-            for depth in range(3):
-                at = tile * TALL + depth * CH
-                block = packed[g, at : at + CH].astype(F32).T
-                low = LANES * tile
-                for pair in range(9):
-                    begin, end = max(low, CH * pair), min(low + LANES, CH * (pair + 1))
-                    if begin < end:
-                        row = (3 * pair + depth) * CH + begin - CH * pair
-                        result[row : row + end - begin] = block[begin - low : end - low]
-
+        for n in blocks:
+            block = packed[g, n * CH : (n + 1) * CH].astype(F32).T
+            low = LANES * (n // 3)
+            for pair in range(9):
+                begin, end = max(low, CH * pair), min(low + LANES, CH * (pair + 1))
+                if begin < end:
+                    row = (3 * pair + n % 3) * CH + begin - CH * pair
+                    result[row : row + end - begin] = block[begin - low : end - low]
+
+    gradient(ct, bh, 1, 0, False)
+    core_send(1)
+    through((0, 15))
+    turn(slopes, 0, st, (0, 7))
     gradient(st, bx, 0, 1, False)
     core_send(0)
-    gradient(ct, bh, 1, 0, False)
-    core_send(1)
+    core_add(1)
     core_add(0)
-    core_add(1)
 
     for planes in ((0, 1, 2, 3), (4, 5, 6, 7), (8, 9, 10, 11), (12, 13, 14, 15)):
         start, count = planes[0], len(planes)
@@ -412,7 +422,7 @@
     lax.fori_loop(0, 2, place, 0, unroll=True)
 
     for stage in (plane_add, line_add, plane_gather, core_gather):
-        for g in range(2):
+        for g in (1, 0):
             stage(g)
     for copy in sent:
         copy.wait_send()

time: 49.4 us -> 49.7 us (level)
  no operation moved by 1% of the time
where the time goes in v7:
time: 49.7 us; the launch traced here: 49.6 us
  Pallas kernels  47.6 us (96%)
  between operations  1.93 us (4%)
    pallas_call x1, Pallas kernels, on_device(): pl.pallas_call(functools.partial(section, scale), out_shape=results, in_s...  46 us
    pallas_call x1, Pallas kernels, on_device(): pl.pallas_call(store, out_shape=results, in_specs=[vmem] * 3, out_specs=(...  1.61 us

profile of v7, /device:TPU:1, one launch (start us, length us, event | category | flops | bytes accessed | tf_op | source)
XLA Modules:
  0.0 49.6 jit_solution(15213494925244458839)
XLA Ops:
  1.9 46.0 %section.1 = (bf16[2,8,8,8,96]{4,3,2,1,0:T(8,128)(2,1)S(1)}, f32[2592,96]{1,0:T(8,128)S(1)}, f32[2592,96]{1,0:T(8,128)S(1)}) custom-call(s32[1,1]{1,0:T(1,128)S(6)} %copy.10.down_ref, s32[1,1]{1,0:T(1,128)S(6)} %copy.9.up_ref, bf16[2,8,8,8,96]{4,3,2,1,0:T(8,128)(2,1)} %bitcast.5, bf16[2,8,8,8,96]{4,3,2,1,0:T(8,128)(2,1)} %bitcast.6, ...), custom_call_target="tpu_custom_call" | custom-call | tf_op jit(solution)/shard_map/section/pallas_call | solution.py:461
  48.0 1.6 %store.1 = (bf16[2,8,8,8,96]{4,3,2,1,0:T(8,128)(2,1)}, f32[2592,96]{1,0:T(8,128)}, f32[2592,96]{1,0:T(8,128)}) custom-call(bf16[2,8,8,8,96]{4,3,2,1,0:T(8,128)(2,1)S(1)} %get-tuple-element.9.refs_0_, f32[2592,96]{1,0:T(8,128)S(1)} %get-tuple-element.10.refs_1_, f32[2592,96]{1,0:T(8,128)S(1)} %get-tuple-element.11.refs_2_), custom_call_target="tpu_custom_call" | custom-call | tf_op jit(solution)/shard_map/store/pallas_call | solution.py:491

commit v8 on v6

--- a/solution.py
+++ b/solution.py
@@ -320,7 +320,7 @@
             start = lax.rem(my_x + a, SIZE_X) * GROUP
             src = part_sum.at[g, rows_of((1 - core) * HALF + start, GROUP)]
             dst = core_in.at[g, rows_of(start, GROUP)]
-            sent.append(send(src, dst, s0.at[g, a], r0.at[g, a], twin))
+            send(src, dst, s0.at[g], r0.at[g, a], twin)
 
     def all_sent(src, sem):
         pltpu.make_async_copy(src, src, sem).wait()
@@ -330,7 +330,7 @@
             x, t = moved(a, b)
             if b == STEPS[0]:
                 group = core_in.at[g, rows_of(x * GROUP, GROUP)]
-                arrived(group, s0.at[g, a], r0.at[g, a], twin)
+                arrived(group, s0.at[g], r0.at[g, a], twin)
             at = x * GROUP + t * SHARD
             total = part_sum[g, rows_of(core * HALF + at, SHARD)] + core_in[g, rows_of(at, SHARD)]
             plane_out[g, n] = total.astype(BF16)
@@ -356,11 +356,10 @@
         rows = rows_of(core * HALF + my_x * GROUP + side * SHARD, SHARD)
         packed[g, rows] = (total * scale).astype(BF16)
         mine = packed.at[g, rows]
-        me = side * SIZE_X + my_x
-        for k in range(SIDE * SIZE_X - 1):
-            at = other(k, me)
-            target = in_plane(lax.rem(at, SIZE_X), lax.div(at, SIZE_X))
-            send(mine, mine, s3.at[g], r3.at[g, my_x], target)
+        for t in range(SIDE):
+            for a in STEPS_X[: 3 + (t < SIDE - 1)]:
+                target = in_plane(moved(a, 0)[0], t if a else other(t, side))
+                send(mine, mine, s3.at[g], r3.at[g, my_x], target)
 
     def plane_gather(g):
         for a in STEPS_X[::-1]:
@@ -368,13 +367,13 @@
             count = GROUP if a else GROUP - SHARD
             arrived(packed.at[g, rows_of(core * HALF + x * GROUP, count)], s3.at[g], r3.at[g, x], twin)
             group = packed.at[g, rows_of(core * HALF + x * GROUP, GROUP)]
-            sent.append(send(group, group, s4.at[g, a], r4.at[g, a], twin))
+            send(group, group, s4.at[g], r4.at[g, a], twin)
 
     def core_gather(g):
         for a in STEPS_X[::-1]:
             x = lax.rem(my_x + SIZE_X - a, SIZE_X)
             group = packed.at[g, rows_of((1 - core) * HALF + x * GROUP, GROUP)]
-            arrived(group, s4.at[g, a], r4.at[g, a], twin)
+            arrived(group, s4.at[g], r4.at[g, a], twin)
         result = (grad_first, grad_second)[g]
         for tile in range(TILES_WIDE):
             for depth in range(3):
@@ -417,9 +416,11 @@
     for copy in sent:
         copy.wait_send()
     for g in range(2):
+        all_sent(part_sum.at[g, :HALF], s0.at[g])
         all_sent(plane_out.at[g], s1.at[g])
         all_sent(cross.at[g, : SIDE - 1], s2.at[g])
         all_sent(packed.at[g, : HALF - SHARD], s3.at[g])
+        all_sent(packed.at[g, :HALF], s4.at[g])
 
 
 def store(*refs):
@@ -465,7 +466,7 @@
             pltpu.VMEM((2, SIDE, SHARD, LANES), F32),
             pltpu.VMEM((2, 2 * HALF, LANES), BF16),
             dma((4,)), dma((2,)), dma((2,)),
-            *[dma((2, SIZE_X))] * 2, *[dma((2,))] * 5, *[dma((2, SIZE_X))] * 3,
+            dma((2,)), dma((2, SIZE_X)), *[dma((2,))] * 5, dma((2, SIZE_X)), dma((2,)), dma((2, SIZE_X)),
         ],
         compiler_params=pltpu.CompilerParams(
             collective_id=0, has_side_effects=True, vmem_limit_bytes=48 * 2**20

time: 49.4 us -> 49.2 us (level)
  no operation moved by 1% of the time
where the time goes in v8:
time: 49.2 us; the launch traced here: 49.1 us
  Pallas kernels  47.1 us (96%)
  between operations  1.93 us (4%)
    pallas_call x1, Pallas kernels, on_device(): pl.pallas_call(functools.partial(section, scale), out_shape=results, in_s...  45.5 us
    pallas_call x1, Pallas kernels, on_device(): pl.pallas_call(store, out_shape=results, in_specs=[vmem] * 3, out_specs=(...  1.61 us

profile of v8, /device:TPU:1, one launch (start us, length us, event | category | flops | bytes accessed | tf_op | source)
XLA Modules:
  0.0 49.1 jit_solution(15854207368538068752)
XLA Ops:
  1.9 45.5 %section.1 = (bf16[2,8,8,8,96]{4,3,2,1,0:T(8,128)(2,1)S(1)}, f32[2592,96]{1,0:T(8,128)S(1)}, f32[2592,96]{1,0:T(8,128)S(1)}) custom-call(s32[1,1]{1,0:T(1,128)S(6)} %copy.10.down_ref, s32[1,1]{1,0:T(1,128)S(6)} %copy.9.up_ref, bf16[2,8,8,8,96]{4,3,2,1,0:T(8,128)(2,1)} %bitcast.5, bf16[2,8,8,8,96]{4,3,2,1,0:T(8,128)(2,1)} %bitcast.6, ...), custom_call_target="tpu_custom_call" | custom-call | tf_op jit(solution)/shard_map/section/pallas_call | solution.py:452
  47.5 1.6 %store.1 = (bf16[2,8,8,8,96]{4,3,2,1,0:T(8,128)(2,1)}, f32[2592,96]{1,0:T(8,128)}, f32[2592,96]{1,0:T(8,128)}) custom-call(bf16[2,8,8,8,96]{4,3,2,1,0:T(8,128)(2,1)S(1)} %get-tuple-element.9.refs_0_, f32[2592,96]{1,0:T(8,128)S(1)} %get-tuple-element.10.refs_1_, f32[2592,96]{1,0:T(8,128)S(1)} %get-tuple-element.11.refs_2_), custom_call_target="tpu_custom_call" | custom-call | tf_op jit(solution)/shard_map/store/pallas_call | solution.py:482
